TPU v7x, 256 devices: a whole 4x4x8 slice. The times are simulated.
256 devices in a mesh: row: 8 (over z_lo, x), col: 32 (over z_hi, y, core).
Axes of the slice: x: 4, y: 4, z: 8 (z_hi: 4, z_lo: 2; z = z_hi * 2 + z_lo), core: 2. Of those that a mesh axis runs over, the one named last changes fastest.
Arguments:
- pair: bfloat16 [1024, 1024, 128], P('row', 'col'), may hold values from -6 to 6
- in_gain: float32 [2, 128], replicated, may hold values from 0.1 to 1.9
- w_in: bfloat16 [2, 128, 512], replicated, may hold values from -0.5 to 0.5
- out_gain: float32 [2, 128], replicated, may hold values from 0.1 to 1.9
- out_bias: float32 [2, 128], replicated, may hold values from -3 to 3
- w_out: bfloat16 [2, 128, 128], replicated, may hold values from -0.5 to 0.5
- w_gate_out: bfloat16 [2, 128, 128], replicated, may hold values from -0.5 to 0.5
Outputs:
- updated: bfloat16 [1024, 1024, 128], P('row', 'col')
All inputs are finite; a program needn't handle non-finite values.
Results may differ from a plain program's by a relative error of at most 0.015.
Values may be sent and summed in bfloat16 or wider, within the bound.
A program may use at most 64 MiB of HBM per device.

v0:
```python
import jax
import jax.numpy as jnp
from jax import lax
from jax.sharding import PartitionSpec as P

EPS = 1e-05


def layer_norm(values, gain, bias, axis):
    mean = jnp.mean(values, axis=axis, keepdims=True)
    var = jnp.mean(jnp.square(values - mean), axis=axis, keepdims=True)
    return (values - mean) * lax.rsqrt(var + EPS) * gain + bias


def triangle(block, index, in_gain, w_in, out_gain, out_bias, w_out, w_gate_out):
    hidden = w_out.shape[1]
    x = layer_norm(block.astype(jnp.float32), in_gain[index], 0.0, -1).astype(jnp.bfloat16)
    mixed = jnp.einsum("itc,cd->dti", x, w_in[index], preferred_element_type=jnp.float32)
    left = (mixed[0:hidden] * jax.nn.sigmoid(mixed[2 * hidden : 3 * hidden])).astype(jnp.bfloat16)
    right = (mixed[hidden : 2 * hidden] * jax.nn.sigmoid(mixed[3 * hidden : 4 * hidden])).astype(
        jnp.bfloat16
    )
    left_panel, right_panel = (
        lax.all_to_all(left, "col", split_axis=0, concat_axis=1, tiled=True),
        lax.all_to_all(right, "col", split_axis=0, concat_axis=1, tiled=True),
    )
    rows = left_panel.shape[2]
    if index == 0:
        product = jnp.einsum(
            "ckj,cki->cji",
            lax.all_gather(right_panel, "row", axis=2, tiled=True),
            left_panel,
            preferred_element_type=jnp.float32,
        )
    else:
        offset = lax.axis_index("row") * rows
        left_piece = lax.all_gather(left_panel, "row", axis=2, tiled=True)
        right_piece = lax.all_gather(right_panel, "row", axis=2, tiled=True)
        sliced = lax.dynamic_slice_in_dim(left_piece, offset, rows, 1)
        product = jnp.einsum(
            "cjk,cik->cji", right_piece, sliced, preferred_element_type=jnp.float32
        )
    home = lax.all_to_all(
        product.astype(jnp.bfloat16), "col", split_axis=1, concat_axis=0, tiled=True
    ).astype(product.dtype)
    normed = layer_norm(
        home, out_gain[index][:, None, None], out_bias[index][:, None, None], 0
    ).astype(jnp.bfloat16)
    projected = jnp.einsum("dji,dc->ijc", normed, w_out[index], preferred_element_type=jnp.float32)
    gate = jnp.einsum("itc,cd->itd", x, w_gate_out[index], preferred_element_type=jnp.float32)
    return (block.astype(jnp.float32) + projected * jax.nn.sigmoid(gate)).astype(jnp.bfloat16)


def local(pair, in_gain, w_in, out_gain, out_bias, w_out, w_gate_out):
    first = triangle(pair, 0, in_gain, w_in, out_gain, out_bias, w_out, w_gate_out)
    return triangle(first, 1, in_gain, w_in, out_gain, out_bias, w_out, w_gate_out)


def solution(mesh):
    in_specs = (P("row", "col", None), P(), P(), P(), P(), P(), P())
    out_specs = P("row", "col", None)
    return jax.shard_map(local, mesh=mesh, in_specs=in_specs, out_specs=out_specs, check_vma=False)
```

profile of v0, /device:TPU:1, one launch (start us, length us, event | category | flops | bytes accessed | tf_op | source)
XLA Modules:
  0.0 536.4 jit_solution(10681431630511754529)
XLA Ops:
  6.5 2.0 copy.75
  8.5 0.2 convert_reduce_fusion.1
  8.7 0.3 fusion.7
  9.1 1.4 convolution_bitcast_fusion.1
  10.5 1.1 fusion.45
  11.6 1.7 copy.77
  13.3 40.4 %all_to_all.90 = bf16[128,32,128]{2,1,0:T(8,128)(2,1)S(1)} all-to-all(bf16[128,32,128]{2,1,0:T(8,128)(2,1)} %copy.77), channel_id=1, replica_groups=mesh['row'=8,'col'=32] {'col'}, dimensions={0} | all-to-all | bytes 2097152 | tf_op jit(solution)/shard_map/all_to_all | solution.py:25
  53.8 1.3 copy.79
  55.1 1.0 copy.80
  56.1 44.8 %all_to_all.91 = bf16[128,32,128]{2,1,0:T(8,128)(2,1)S(1)} all-to-all(bf16[128,32,128]{2,1,0:T(8,128)(2,1)S(1)} %copy.80), channel_id=1, replica_groups=mesh['row'=8,'col'=32] {'col'}, dimensions={0} | all-to-all | bytes 2097152 | tf_op jit(solution)/shard_map/all_to_all | solution.py:24
  101.0 66.8 %all-gather.4.cloned.1.call-done = bf16[4,1024,1024]{1,2,0:T(8,128)(2,1)} async-done(((bf16[4,1024,128]{1,2,0:T(8,128)(2,1)}), bf16[4,1024,1024]{1,2,0:T(8,128)(2,1)}) %all-gather.4.cloned.1.call-update) | async-done | bytes 8388624 | tf_op jit(solution)/shard_map/all_gather | solution.py:31
  167.8 5.7 %convolution_convert_fusion.1 = bf16[4,1024,128]{2,1,0:T(8,128)(2,1)S(1)} fusion(bf16[4,1024,1024]{1,2,0:T(8,128)(2,1)} %all-gather.4.cloned.1.call-done, bf16[4,1024,128]{2,1,0:T(8,128)(2,1)S(1)} %bitcast.121), kind=kOutput, calls=%fused_computation.65 | convolution fusion | flops 1074266112 | bytes 10485760 | tf_op jit(solution)/shard_map/ckj,cki->cji/dot_general | solution.py:29
  173.5 1.8 copy.82
  175.3 9.8 %all-to-all-start.2 = ((bf16[4,1024,128]{2,0,1:T(4,128)(2,1)}), bf16[4,1024,128]{2,0,1:T(4,128)(2,1)S(1)}, u32[]{:S(2)}, u32[]{:S(2)}) async-start(bf16[4,1024,128]{2,0,1:T(4,128)(2,1)} %copy.82), calls=%async_computation.2 | async-start | bytes 2097152 | tf_op jit(solution)/shard_map/all_to_all | solution.py:43
  185.2 0.2 all-gather.6.cloned.1.call-start
  185.5 0.1 mul.106
  185.6 28.3 %all-to-all-done.2 = bf16[4,1024,128]{2,0,1:T(4,128)(2,1)S(1)} async-done(((bf16[4,1024,128]{2,0,1:T(4,128)(2,1)}), bf16[4,1024,128]{2,0,1:T(4,128)(2,1)S(1)}, u32[]{:S(2)}, u32[]{:S(2)}) %all-to-all-start.2) | async-done | bytes 1048608 | tf_op jit(solution)/shard_map/all_to_all | solution.py:43
  213.9 0.5 fusion.37
  214.4 0.7 fusion.40
  215.1 1.0 fusion.43
  216.1 0.5 copy.83
  216.7 0.5 fusion.60
  217.1 0.4 copy-done.5
  217.5 1.2 convert_reduce_fusion
  218.7 0.4 fusion.4
  219.1 1.4 convolution_bitcast_fusion
  220.4 1.1 fusion.47
  221.5 1.7 copy.88
  223.2 34.3 %all_to_all.92 = bf16[128,32,128]{2,1,0:T(8,128)(2,1)S(1)} all-to-all(bf16[128,32,128]{2,1,0:T(8,128)(2,1)} %copy.88), channel_id=1, replica_groups=mesh['row'=8,'col'=32] {'col'}, dimensions={0} | all-to-all | bytes 2097152 | tf_op jit(solution)/shard_map/all_to_all | solution.py:25
  257.5 1.1 copy.89
  258.7 1.0 copy.90
  259.7 44.0 %all_to_all.93 = bf16[128,32,128]{2,1,0:T(8,128)(2,1)S(1)} all-to-all(bf16[128,32,128]{2,1,0:T(8,128)(2,1)S(1)} %copy.90), channel_id=1, replica_groups=mesh['row'=8,'col'=32] {'col'}, dimensions={0} | all-to-all | bytes 2097152 | tf_op jit(solution)/shard_map/all_to_all | solution.py:24
  303.6 1.1 copy.91
  304.8 69.4 %all-gather.6.cloned.1.call-done = bf16[4,1024,1024]{2,1,0:T(8,128)(2,1)} async-done(((bf16[4,1024,128]{2,1,0:T(8,128)(2,1)}), bf16[4,1024,1024]{2,1,0:T(8,128)(2,1)}) %all-gather.6.cloned.1.call-update) | async-done | bytes 8388624 | tf_op jit(solution)/shard_map/all_gather | solution.py:38
  374.2 101.6 %all-gather.8.cloned.1.call-done = bf16[4,1024,1024]{2,1,0:T(8,128)(2,1)} async-done(((bf16[4,1024,128]{2,1,0:T(8,128)(2,1)}), bf16[4,1024,1024]{2,1,0:T(8,128)(2,1)}) %all-gather.8.cloned.1.call-update) | async-done | bytes 8388624 | tf_op jit(solution)/shard_map/all_gather | solution.py:37
  475.8 5.9 %convolution_convert_fusion = bf16[4,1024,128]{2,1,0:T(8,128)(2,1)S(1)} fusion(bf16[4,1024,1024]{2,1,0:T(8,128)(2,1)} %all-gather.6.cloned.1.call-done, bf16[4,1024,1024]{2,1,0:T(8,128)(2,1)} %all-gather.8.cloned.1.call-done, s32[]{:T(128)S(6)} %select_n.3), kind=kOutput, calls=%fused_computation.64 | convolution fusion | flops 1074266112 | bytes 10485764 | tf_op jit(solution)/shard_map/cjk,cik->cji/dot_general | solution.py:40
  481.7 1.8 copy.92
  483.5 13.3 %all-to-all-start.5 = ((bf16[4,1024,128]{2,0,1:T(4,128)(2,1)}), bf16[4,1024,128]{2,0,1:T(4,128)(2,1)S(1)}, u32[]{:S(2)}, u32[]{:S(2)}) async-start(bf16[4,1024,128]{2,0,1:T(4,128)(2,1)} %copy.92), calls=%async_computation.5 | async-start | bytes 2097152 | tf_op jit(solution)/shard_map/all_to_all | solution.py:43
  496.9 0.1 add.95
  497.1 28.3 %all-to-all-done.5 = bf16[4,1024,128]{2,0,1:T(4,128)(2,1)S(1)} async-done(((bf16[4,1024,128]{2,0,1:T(4,128)(2,1)}), bf16[4,1024,128]{2,0,1:T(4,128)(2,1)S(1)}, u32[]{:S(2)}, u32[]{:S(2)}) %all-to-all-start.5) | async-done | bytes 1048608 | tf_op jit(solution)/shard_map/all_to_all | solution.py:43
  525.4 0.1 copy.93
  525.6 0.2 fusion.29
  525.8 0.3 fusion.32
  526.1 0.4 fusion.35
  526.6 0.1 copy.96
  526.7 0.5 fusion.48
  527.2 1.0 fusion.11
  528.2 1.7 copy.101
  (32 shorter events, 0.7 us)
Async XLA Ops:
  6.5 2.6 copy-start.2
  6.5 2.6 copy-start
  6.5 161.3 %all-gather.4.cloned.1.call-start = ((), (), s32[]{:S(2)}) async-start(), calls=%async_computation.6 | async-start | bytes 9437184 | tf_op jit(solution)/shard_map/all_gather | solution.py:31
  173.5 11.9 %copy-start.3 = (f32[2,128]{1,0:T(2,128)S(1)}, f32[2,128]{1,0:T(2,128)}, u32[]{:S(2)}) copy-start(f32[2,128]{1,0:T(2,128)} %param.11) | copy-start | bytes 3076
  173.5 11.9 %copy-start.4 = (f32[2,128]{1,0:T(2,128)S(1)}, f32[2,128]{1,0:T(2,128)}, u32[]{:S(2)}) copy-start(f32[2,128]{1,0:T(2,128)} %param.10) | copy-start | bytes 3076
  175.3 38.6 %all-to-all-start.2 = ((bf16[4,1024,128]{2,0,1:T(4,128)(2,1)}), bf16[4,1024,128]{2,0,1:T(4,128)(2,1)S(1)}, u32[]{:S(2)}, u32[]{:S(2)}) async-start(bf16[4,1024,128]{2,0,1:T(4,128)(2,1)} %copy.82), calls=%async_computation.2 | async-start | bytes 2097152 | tf_op jit(solution)/shard_map/all_to_all | solution.py:43
  185.2 189.0 %all-gather.6.cloned.1.call-start = ((), (), s32[]{:S(2)}) async-start(), calls=%async_computation.7 | async-start | bytes 9437184 | tf_op jit(solution)/shard_map/all_gather | solution.py:38
  215.1 1.5 copy-start.1
  216.6 0.8 copy-start.5
  258.6 217.1 %all-gather.8.cloned.1.call-start = ((), (), s32[]{:S(2)}) async-start(), calls=%async_computation.8 | async-start | bytes 9437184 | tf_op jit(solution)/shard_map/all_gather | solution.py:37
  483.5 42.0 %all-to-all-start.5 = ((bf16[4,1024,128]{2,0,1:T(4,128)(2,1)}), bf16[4,1024,128]{2,0,1:T(4,128)(2,1)S(1)}, u32[]{:S(2)}, u32[]{:S(2)}) async-start(bf16[4,1024,128]{2,0,1:T(4,128)(2,1)} %copy.92), calls=%async_computation.5 | async-start | bytes 2097152 | tf_op jit(solution)/shard_map/all_to_all | solution.py:43
Sparse Core Ops, SparseCore 0:
  55.2 112.5 all-gather.3
  258.8 115.3 all-gather.5
  375.9 99.8 all-gather.7
where the time goes:
time: 537 us; the launch traced here: 536 us
  waiting for transfers between devices  294 us (55%)
  blocking collectives  164 us (31%)
  starting transfers between devices  23.4 us (4%)
  local copies, waits for them, and re-layouts  17.9 us (3%)
  matrix products  17.6 us (3%)
  between operations  13.4 us (2%)
  other arithmetic  6.21 us (1%)
    all_gather x1, waiting for transfers between devices, triangle(): left_piece = lax.all_gather(left_panel, 'row', axis=2, tiled=True)  102 us
    all_to_all x2, blocking collectives, triangle(): lax.all_to_all(left, 'col', split_axis=0, concat_axis=1, tiled=True)  88.8 us
    all_to_all x2, blocking collectives, triangle(): lax.all_to_all(right, 'col', split_axis=0, concat_axis=1, tiled=True)  74.7 us
    all_gather x1, waiting for transfers between devices, triangle(): right_piece = lax.all_gather(right_panel, 'row', axis=2, tiled=True)  69.4 us
    all_gather x1, waiting for transfers between devices, triangle(): lax.all_gather(right_panel, 'row', axis=2, tiled=True)  66.8 us
    all_to_all x2, waiting for transfers between devices, triangle(): lax.all_to_all(product.astype(jnp.bfloat16), 'col', split_axis=1, concat_...  56.6 us
    all_to_all x2, starting transfers between devices, triangle(): lax.all_to_all(product.astype(jnp.bfloat16), 'col', split_axis=1, concat_...  23.1 us
  transfers between devices with their start and end apart: 5, of which 5 were waited for; matrix products, arithmetic and copies ran while one was open for 1% of the time, Pallas kernels for 0%

commit v1 on v0

--- a/solution.py
+++ b/solution.py
@@ -1,9 +1,181 @@
+import functools
+
 import jax
 import jax.numpy as jnp
 from jax import lax
+from jax.experimental import pallas as pl
+from jax.experimental.pallas import tpu as pltpu
 from jax.sharding import PartitionSpec as P
 
 EPS = 1e-05
+MESH = pl.DeviceIdType.MESH
+CHIPS = 128
+
+
+def chip_of(x, y, z):
+    return x * 32 + y * 8 + z
+
+
+def coordinates():
+    row, col = lax.axis_index("row"), lax.axis_index("col")
+    return row % 4, (col // 2) % 4, row // 4, col // 8, col % 2
+
+
+def device(x, y, z_lo, z_hi, core):
+    return z_lo * 4 + x, z_hi * 8 + y * 2 + core
+
+
+def exchange_kernel(update, ab, home, panel, swap_b, swap_a, product, sems):
+    send, recv, back_send, back_recv = [sems.at[n] for n in range(4)]
+    bar = pltpu.get_barrier_semaphore()
+    x, y, z_lo, z_hi, core = coordinates()
+    z = z_hi * 2 + z_lo
+    mine = chip_of(x, y, z)
+    row, col = lax.axis_index("row"), lax.axis_index("col")
+    partner = device(x, y, z_lo, z_hi, 1 - core)
+    straight = core == z_lo
+
+    def home_target(s):
+        to_x, to_y = (x + s // 32) % 4, (y + (s // 8) % 4) % 4
+        return to_x, to_y, (z_hi + (s // 2) % 4) % 4, (core + s) % 2
+
+    def greet(s, _):
+        to_x, to_y, to_z, to_core = home_target(s)
+        to = device(to_x, to_y, core, to_z, to_core)
+
+        @pl.when(jnp.logical_not(jnp.logical_and(s == 0, straight)))
+        def _():
+            pl.semaphore_signal(bar, inc=1, device_id=to, device_id_type=MESH)
+
+        return 0
+
+    lax.fori_loop(0, CHIPS, greet, 0)
+
+    @pl.when(jnp.logical_not(straight))
+    def _():
+        pl.semaphore_signal(bar, inc=1, device_id=partner, device_id_type=MESH)
+
+    pl.semaphore_wait(bar, CHIPS)
+
+    def spread(s, _):
+        to_x, to_y, to_z = (x + s // 32) % 4, (y + (s // 8) % 4) % 4, (z + s) % 8
+        channel = chip_of(to_x, to_y, to_z)
+
+        @pl.when(jnp.logical_and(s == 0, straight))
+        def _():
+            pltpu.make_async_copy(ab.at[channel], panel.at[col, x], recv).start()
+
+        @pl.when(jnp.logical_not(jnp.logical_and(s == 0, straight)))
+        def _():
+            pltpu.make_async_remote_copy(
+                ab.at[channel],
+                panel.at[col, x],
+                send,
+                recv,
+                device_id=device(to_x, to_y, to_z % 2, to_z // 2, z_lo),
+                device_id_type=MESH,
+            ).start()
+
+        return 0
+
+    lax.fori_loop(0, CHIPS, spread, 0)
+    pltpu.make_async_copy(panel, panel, recv).wait()
+
+    def swap(source, target, at):
+        return pltpu.make_async_remote_copy(
+            source, target, sems.at[4 + at], sems.at[6 + at], device_id=partner, device_id_type=MESH
+        )
+
+    swaps = [swap(panel.at[:, :, 1], swap_b, 0)]
+    if update == 1:
+        swaps.append(swap(panel.at[pl.ds(16 * (1 - core), 16), :, 0], swap_a, 1))
+    for copy in swaps:
+        copy.start()
+    for copy in swaps:
+        copy.wait()
+
+    if update == 0:
+        left = jnp.concatenate([panel[:, n, 0].reshape(1024, 128) for n in range(4)], axis=1)
+        for half, source in ((core, panel.at[:, :, 1]), (1 - core, swap_b)):
+            right = jnp.concatenate([source[:, n].reshape(1024, 128) for n in range(4)], axis=1)
+            out = lax.dot_general(
+                right, left, (((0,), (0,)), ((), ())), preferred_element_type=jnp.float32
+            ).astype(jnp.bfloat16)
+            for n in range(4):
+                product[pl.ds(16 * half, 16), n] = out[:, 128 * n : 128 * n + 128].reshape(16, 32, 128)
+    else:
+        own = pl.ds(16 * core, 16)
+        left = jnp.concatenate(
+            [panel[own, n, 0].reshape(512, 128) for n in range(4)]
+            + [swap_a[:, n].reshape(512, 128) for n in range(4)],
+            axis=1,
+        )
+        for half in range(2):
+            part = slice(16 * half, 16 * half + 16)
+            right = jnp.concatenate(
+                [panel[part, n, 1].reshape(512, 128) for n in range(4)]
+                + [swap_b[part, n].reshape(512, 128) for n in range(4)],
+                axis=1,
+            )
+            out = lax.dot_general(
+                right, left, (((1,), (1,)), ((), ())), preferred_element_type=jnp.float32
+            ).astype(jnp.bfloat16)
+            for n in range(4):
+                product[part, n] = out[:, 128 * n : 128 * n + 128].reshape(16, 32, 128)
+
+    def give_back(s, _):
+        to_x, to_y, to_z, to_core = home_target(s)
+        to = device(to_x, to_y, core, to_z, to_core)
+
+        @pl.when(jnp.logical_and(s == 0, straight))
+        def _():
+            pltpu.make_async_copy(product.at[to[1], to_x], home.at[mine], back_recv).start()
+
+        @pl.when(jnp.logical_not(jnp.logical_and(s == 0, straight)))
+        def _():
+            pltpu.make_async_remote_copy(
+                product.at[to[1], to_x],
+                home.at[mine],
+                back_send,
+                back_recv,
+                device_id=to,
+                device_id_type=MESH,
+            ).start()
+
+        return 0
+
+    lax.fori_loop(0, CHIPS, give_back, 0)
+    pltpu.make_async_copy(home, home, back_recv).wait()
+
+    rest = ab.at[pl.ds(0, CHIPS - 1)], home.at[pl.ds(0, CHIPS - 1)]
+    pltpu.make_async_copy(rest[0], rest[0], send).wait()
+    pltpu.make_async_copy(rest[1], rest[1], back_send).wait()
+
+    @pl.when(jnp.logical_not(straight))
+    def _():
+        pltpu.make_async_copy(ab.at[0], ab.at[0], send).wait()
+        pltpu.make_async_copy(home.at[0], home.at[0], back_send).wait()
+
+
+def exchange(ab, update):
+    vmem = pl.BlockSpec(memory_space=pltpu.VMEM)
+    return pl.pallas_call(
+        functools.partial(exchange_kernel, update),
+        out_shape=jax.ShapeDtypeStruct((CHIPS, 32, 128), jnp.bfloat16),
+        in_specs=[vmem],
+        out_specs=vmem,
+        scratch_shapes=[
+            pltpu.VMEM((32, 4, 2, 32, 128), jnp.bfloat16),
+            pltpu.VMEM((32, 4, 32, 128), jnp.bfloat16),
+            pltpu.VMEM((16, 4, 32, 128), jnp.bfloat16),
+            pltpu.VMEM((32, 4, 32, 128), jnp.bfloat16),
+            pltpu.SemaphoreType.DMA((8,)),
+        ],
+        compiler_params=pltpu.CompilerParams(
+            collective_id=update, has_side_effects=True, vmem_limit_bytes=32 << 20
+        ),
+        name=f"exchange{update}",
+    )(ab)
 
 
 def layer_norm(values, gain, bias, axis):
@@ -20,29 +192,7 @@
     right = (mixed[hidden : 2 * hidden] * jax.nn.sigmoid(mixed[3 * hidden : 4 * hidden])).astype(
         jnp.bfloat16
     )
-    left_panel, right_panel = (
-        lax.all_to_all(left, "col", split_axis=0, concat_axis=1, tiled=True),
-        lax.all_to_all(right, "col", split_axis=0, concat_axis=1, tiled=True),
-    )
-    rows = left_panel.shape[2]
-    if index == 0:
-        product = jnp.einsum(
-            "ckj,cki->cji",
-            lax.all_gather(right_panel, "row", axis=2, tiled=True),
-            left_panel,
-            preferred_element_type=jnp.float32,
-        )
-    else:
-        offset = lax.axis_index("row") * rows
-        left_piece = lax.all_gather(left_panel, "row", axis=2, tiled=True)
-        right_piece = lax.all_gather(right_panel, "row", axis=2, tiled=True)
-        sliced = lax.dynamic_slice_in_dim(left_piece, offset, rows, 1)
-        product = jnp.einsum(
-            "cjk,cik->cji", right_piece, sliced, preferred_element_type=jnp.float32
-        )
-    home = lax.all_to_all(
-        product.astype(jnp.bfloat16), "col", split_axis=1, concat_axis=0, tiled=True
-    ).astype(product.dtype)
+    home = exchange(jnp.stack([left, right], axis=1), index).astype(jnp.float32)
     normed = layer_norm(
         home, out_gain[index][:, None, None], out_bias[index][:, None, None], 0
     ).astype(jnp.bfloat16)

time: 537 us -> 248 us (0.46)
  waiting for transfers between devices: 294 us -> 0 us
  Pallas kernels: 0 us -> 188 us
  blocking collectives: 164 us -> 0 us
  starting transfers between devices: 23.4 us -> 0 us
  between operations: 13.4 us -> 0.2 us
  other arithmetic: 6.21 us -> 17 us
  local copies, waits for them, and re-layouts: 17.9 us -> 27.7 us
    all_gather x3 -> x0, waiting for transfers between devices: 238 us -> none  [the longest x1 102 us: triangle(): left_piece = lax.all_gather(left_panel, 'row', axis=2, tiled=True)]
    pallas_call x0 -> x2, Pallas kernels: none -> 188 us  [exchange(): pl.pallas_call(functools.partial(exchange_kernel, update), out_shape=jax....]
    all_to_all x4 -> x0, blocking collectives: 164 us -> none  [the longest x2 88.8 us: triangle(): lax.all_to_all(left, 'col', split_axis=0, concat_axis=1, tiled=True)]
    all_to_all x2 -> x0, waiting for transfers between devices: 56.6 us -> none  [triangle(): lax.all_to_all(product.astype(jnp.bfloat16), 'col', split_axis=1, concat_...]
    all_to_all x2 -> x0, starting transfers between devices: 23.1 us -> none  [triangle(): lax.all_to_all(product.astype(jnp.bfloat16), 'col', split_axis=1, concat_...]
    dot_general x0 -> x2, local copies, waits for them, and re-layouts: none -> 21.9 us  [triangle(): jnp.einsum('itc,cd->dti', x, w_in[index], preferred_element_type=jnp.floa...]
    dot_general x2 -> x0, matrix products: 11.7 us -> none  [the longest x1 5.95 us: triangle(): jnp.einsum('cjk,cik->cji', right_piece, sliced, preferred_element_type=jn...]
    convert_element_type x7 -> x0, local copies, waits for them, and re-layouts: 10.5 us -> none  [the longest x2 3.56 us: triangle(): product.astype(jnp.bfloat16)]
  transfers between devices with their start and end apart: 5 -> 0, of which waited for: 5 -> 0; matrix products, arithmetic and copies ran while one was open for 1% -> 0% of each run, Pallas kernels for 0% -> 0%
where the time goes in v1:
time: 248 us; the launch traced here: 247 us
  Pallas kernels  188 us (76%)
  local copies, waits for them, and re-layouts  27.7 us (11%)
  other arithmetic  17 us (7%)
  matrix products  14.5 us (6%)
    pallas_call x2, Pallas kernels, exchange(): pl.pallas_call(functools.partial(exchange_kernel, update), out_shape=jax....  188 us
    dot_general x2, local copies, waits for them, and re-layouts, triangle(): jnp.einsum('itc,cd->dti', x, w_in[index], preferred_element_type=jnp.floa...  21.9 us
    another operation x4, other arithmetic, triangle(): home = exchange(jnp.stack([left, right], axis=1), index).astype(jnp.float32)  9.58 us
    dot_general x2, matrix products, triangle(): jnp.einsum('itc,cd->dti', x, w_in[index], preferred_element_type=jnp.floa...  7.98 us

profile of v1, /device:TPU:1, one launch (start us, length us, event | category | flops | bytes accessed | tf_op | source)
XLA Modules:
  0.0 247.2 jit_solution(16290421259327683800)
XLA Ops:
  0.0 0.0 copy-start
  0.0 0.0 copy-start.1
  0.0 0.8 slice_bitcast_fusion.2
  0.8 0.8 slice_bitcast_fusion
  1.6 1.8 convert_reduce_fusion.1
  3.4 2.3 fusion.11
  5.8 0.0 copy-done
  5.8 0.0 copy-done.1
  5.8 4.0 %fusion.52 = f32[128,32,512]{2,1,0:T(8,128)} fusion(bf16[128,32,128]{2,1,0:T(8,128)(2,1)S(1)} %copy-done, f32[128]{0:T(128)S(1)} %get-tuple-element.14, f32[128,32]{1,0:T(8,128)S(1)} %add_rsqrt_fusion.1, f32[128,32]{1,0:T(8,128)S(1)} %broadcast_multiply_fusion.1, bf16[2,128,512]{2,1,0:T(8,128)(2,1)S(1)} %copy-done.1), kind=kOutput, calls=%fused_computation.67 | convolution fusion | flops 539492352 | bytes 9699840 | tf_op jit(solution)/shard_map/itc,cd->dti/dot_general | solution.py:190
  9.8 10.9 %copy.9 = f32[128,32,512]{0,1,2:T(8,128)} copy(f32[128,32,512]{2,1,0:T(8,128)} %fusion.52) | data formatting | bytes 16777216 | tf_op jit(solution)/shard_map/itc,cd->dti/dot_general | solution.py:190
  20.7 4.6 %fusion.61 = (bf16[128,1,32,128]{3,2,0,1:T(8,128)(2,1)S(1)}, bf16[128,1,32,128]{3,2,0,1:T(8,128)(2,1)S(1)}) fusion(f32[512,32,128]{2,1,0:T(8,128)} %bitcast.62), kind=kLoop, calls=%fused_computation.75 | loop fusion | flops 5242880 | bytes 10485760 | tf_op jit(solution)/shard_map/stack | solution.py:195
  25.3 0.2 pad_maximum_fusion
  25.5 0.7 copy.10.ab
  26.2 97.2 %exchange0.1 = bf16[128,32,128]{2,1,0:T(8,128)(2,1)S(1)} custom-call(bf16[128,2,32,128]{3,2,1,0:T(8,128)(2,1)S(1)} %copy.10.ab), custom_call_target="tpu_custom_call" | custom-call | tf_op jit(solution)/shard_map/exchange0/pallas_call | solution.py:162
  123.5 0.2 convert_reduce_fusion.3
  123.7 0.3 fusion.18
  124.0 0.4 fusion.21
  124.4 1.5 copy.26
  126.0 0.0 copy-start.3
  126.0 1.2 fusion.67
  127.2 0.0 copy-done.3
  127.2 2.3 convert_reduce_fusion
  129.5 1.3 fusion.8
  130.8 4.0 %fusion.45 = f32[128,32,512]{2,1,0:T(8,128)} fusion(bf16[128,32,128]{2,1,0:T(8,128)(2,1)S(1)} %get-tuple-element.16, f32[128]{0:T(128)S(1)} %get-tuple-element.13, f32[128,32]{1,0:T(8,128)S(1)} %add_rsqrt_fusion, f32[128,32]{1,0:T(8,128)S(1)} %broadcast_multiply_fusion, bf16[2,128,512]{2,1,0:T(8,128)(2,1)S(1)} %copy-done.1), kind=kOutput, calls=%fused_computation.62 | convolution fusion | flops 539492352 | bytes 9699840 | tf_op jit(solution)/shard_map/itc,cd->dti/dot_general | solution.py:190
  134.8 10.9 %copy.18 = f32[128,32,512]{0,1,2:T(8,128)} copy(f32[128,32,512]{2,1,0:T(8,128)} %fusion.45) | data formatting | bytes 16777216 | tf_op jit(solution)/shard_map/itc,cd->dti/dot_general | solution.py:190
  145.8 4.6 %fusion.59 = (bf16[128,1,32,128]{3,2,1,0:T(8,128)(2,1)S(1)}, bf16[128,1,32,128]{3,2,1,0:T(8,128)(2,1)S(1)}) fusion(f32[512,32,128]{2,1,0:T(8,128)} %bitcast.63), kind=kLoop, calls=%fused_computation.73 | loop fusion | flops 5242880 | bytes 10485760 | tf_op jit(solution)/shard_map/stack | solution.py:195
  150.3 0.3 pad_maximum_fusion.1.ab
  150.6 90.6 %exchange1.1 = bf16[128,32,128]{2,1,0:T(8,128)(2,1)S(1)} custom-call(bf16[128,2,32,128]{3,2,1,0:T(8,128)(2,1)S(1)} %pad_maximum_fusion.1.ab), custom_call_target="tpu_custom_call" | custom-call | tf_op jit(solution)/shard_map/exchange1/pallas_call | solution.py:162
  241.2 0.2 convert_reduce_fusion.2
  241.4 0.3 fusion.14
  241.7 0.0 copy-start.2
  241.8 0.4 fusion.17
  242.2 1.5 copy.32
  243.7 0.0 copy-done.2
  243.8 0.0 copy-start.4
  243.8 0.4 fusion.70
  244.2 0.4 copy-done.4
  244.6 2.6 %fusion.23 = bf16[128,32,128]{2,1,0:T(8,128)(2,1)} fusion(bf16[128,32,128]{2,1,0:T(8,128)(2,1)S(1)} %get-tuple-element.16, f32[32,128,128]{2,0,1:T(8,128)S(1)} %fusion.70, f32[128]{0:T(128)S(1)} %get-tuple-element.13, f32[128,32]{1,0:T(8,128)S(1)} %add_rsqrt_fusion, f32[128,32]{1,0:T(8,128)S(1)} %broadcast_multiply_fusion, ...), kind=kOutput, calls=%fused_computation.33 | convolution fusion | flops 140509184 | bytes 5407232 | tf_op jit(solution)/shard_map/itc,cd->itd/dot_general | solution.py:200
  (8 shorter events, 0.1 us)
Async XLA Ops:
  0.0 5.8 %copy-start = (bf16[128,32,128]{2,1,0:T(8,128)(2,1)S(1)}, bf16[128,32,128]{2,1,0:T(8,128)(2,1)}, u32[]{:S(2)}) copy-start(bf16[128,32,128]{2,1,0:T(8,128)(2,1)} %param.7) | copy-start | bytes 3145732
  0.0 5.8 %copy-start.1 = (bf16[2,128,512]{2,1,0:T(8,128)(2,1)S(1)}, bf16[2,128,512]{2,1,0:T(8,128)(2,1)}, u32[]{:S(2)}) copy-start(bf16[2,128,512]{2,1,0:T(8,128)(2,1)} %param.9) | copy-start | bytes 786436
  126.0 1.2 copy-start.3
  241.7 2.0 copy-start.2
  243.8 0.8 copy-start.4

commit v2 on v0

v2 whole, which is shorter than its diff:
```python
import jax
import jax.numpy as jnp
from jax import lax
from jax.experimental import pallas as pl
from jax.experimental.pallas import tpu as pltpu
from jax.sharding import PartitionSpec as P

EPS = 1e-05
MESH = pl.DeviceIdType.MESH
CHIPS = 128
BLOCKS = 8
WIDE = 512

F32, BF16 = jnp.float32, jnp.bfloat16


def coordinates():
    row, col = lax.axis_index("row"), lax.axis_index("col")
    return row % 4, (col // 2) % 4, row // 4, col // 8, col % 2


def device(x, y, z_lo, z_hi, core):
    return z_lo * 4 + x, z_hi * 8 + y * 2 + core


def sigmoid(values):
    return 0.5 * jnp.tanh(0.5 * values) + 0.5


def norm(values):
    mean = jnp.sum(values, axis=0, keepdims=True) * (1.0 / 128)
    centred = values - mean
    var = jnp.sum(centred * centred, axis=0, keepdims=True) * (1.0 / 128)
    return centred * lax.rsqrt(var + EPS)


def wide(column):
    return jnp.concatenate([column] * (WIDE // 128), axis=1)


def kernel(
    pair, in_gain, w_in, out_gain, out_bias, w_out, w_gate, updated,
    rows32, out_rows, z, x_all, gate, staged, total, gains, wt_in, wt_out, wt_gate,
    ab0, ab1, panel0, panel1, swap_b0, swap_b1, swap_a1, product0, product1, home0, home1,
    send_sems, recv_sems, swap_send, swap_recv, back_send, back_recv,
):
    bar = pltpu.get_barrier_semaphore()
    x, y, z_lo, z_hi, core = coordinates()
    z_at = z_hi * 2 + z_lo
    col = lax.axis_index("col")
    partner = device(x, y, z_lo, z_hi, 1 - core)
    straight = core == z_lo

    def home_target(s):
        to_x, to_y = (x + s // 32) % 4, (y + (s // 8) % 4) % 4
        return device(to_x, to_y, core, (z_hi + (s // 2) % 4) % 4, (core + s) % 2)

    def greet(s, _):
        @pl.when(jnp.logical_not(jnp.logical_and(s == 0, straight)))
        def _():
            pl.semaphore_signal(bar, inc=1, device_id=home_target(s), device_id_type=MESH)

        return 0

    lax.fori_loop(0, CHIPS, greet, 0)

    @pl.when(jnp.logical_not(straight))
    def _():
        pl.semaphore_signal(bar, inc=1, device_id=partner, device_id_type=MESH)

    def flip(block):
        return block.astype(F32).T

    def weights(u):
        for kind in range(4):
            turned = flip(w_in[u, :, 128 * kind : 128 * kind + 128]).astype(BF16)
            wt_in[u, :, kind] = turned.reshape(4, 32, 128)
        gains[3 * u] = jnp.broadcast_to(in_gain[u : u + 1, :], (128, 128)).T

    def late_weights(u):
        wt_out[u] = flip(w_out[u]).astype(BF16)
        wt_gate[u] = flip(w_gate[u]).astype(BF16)
        gains[3 * u + 1] = jnp.broadcast_to(out_gain[u : u + 1, :], (128, 128)).T
        gains[3 * u + 2] = jnp.broadcast_to(out_bias[u : u + 1, :], (128, 128)).T

    def take(t):
        return rows32[pl.ds(t, 128, stride=32), :]

    def projections(u, ab, group):
        lhs = wt_in[u, group].reshape(128, 128)

        def block(n, _):
            mixed = jnp.dot(lhs, x_all[n], preferred_element_type=F32)
            gated = mixed[0:64] * sigmoid(mixed[64:128])
            for kind in range(2):
                for q in range(4):
                    staged[pl.ds(kind * 32 + n * 4 + q, 32, stride=64), :] = gated[
                        32 * kind : 32 * kind + 32, 128 * q : 128 * q + 128
                    ]
            return 0

        lax.fori_loop(0, BLOCKS, block, 0)

        def pack(d, _):
            at = pl.multiple_of(d * 256, 256)
            ab[pl.ds(group * 32 + d * 4, 4)] = (
                staged[pl.ds(at, 256), :].astype(BF16).reshape(4, 2, 32, 128)
            )
            return 0

        lax.fori_loop(0, 8, pack, 0)

    def gates(u):
        def block(n, _):
            gate[n] = sigmoid(jnp.dot(wt_gate[u], x_all[n], preferred_element_type=F32))
            return 0

        lax.fori_loop(0, BLOCKS, block, 0)

    def forward(u, ab, panel):
        outer, inner = (y, x) if u == 0 else (x, y)
        slot = panel.at[y, z_hi * 2 + core, x] if u == 0 else panel.at[x, col]
        send, recv = send_sems.at[u], recv_sems.at[u, outer]
        for d in range(4):
            to_outer = (outer + d) % 4
            projections(u, ab, to_outer)
            if u == 0 and d == 0:
                pl.semaphore_wait(bar, CHIPS)

            def spread(s, _, d=d, to_outer=to_outer):
                to_inner, to_z = (inner + s // 8) % 4, (z_at + s) % 8
                channel = to_outer * 32 + to_inner * 8 + to_z
                to_x, to_y = (to_inner, to_outer) if u == 0 else (to_outer, to_inner)

                def remote():
                    pltpu.make_async_remote_copy(
                        ab.at[channel],
                        slot,
                        send,
                        recv,
                        device_id=device(to_x, to_y, to_z % 2, to_z // 2, z_lo),
                        device_id_type=MESH,
                    ).start()

                if d > 0:
                    remote()
                else:
                    own = jnp.logical_and(s == 0, straight)

                    @pl.when(own)
                    def _():
                        pltpu.make_async_copy(ab.at[channel], slot, recv).start()

                    @pl.when(jnp.logical_not(own))
                    def _():
                        remote()

                return 0

            lax.fori_loop(0, 32, spread, 0)

    def swap(u, chunk, source, target, at):
        return pltpu.make_async_remote_copy(
            source,
            target,
            swap_send.at[u, at, chunk],
            swap_recv.at[u, at, chunk],
            device_id=partner,
            device_id_type=MESH,
        )

    def lanes(parts):
        return jnp.concatenate(parts, axis=1)

    def multiply0(panel, swap_b, product):
        for d in range(4):
            at = (y + 4 - d) % 4
            pltpu.make_async_copy(panel.at[at], panel.at[at], recv_sems.at[0, at]).wait()
            copy = swap(0, at, panel.at[at, :, :, 1], swap_b.at[at], 0)
            copy.start()
            left = lanes([panel[at, :, n, 0].reshape(256, 128) for n in range(4)])
            for side in range(2):
                if side == 0:
                    right = lanes([panel[at, :, n, 1].reshape(256, 128) for n in range(4)])
                else:
                    copy.wait()
                    right = lanes([swap_b[at, :, n].reshape(256, 128) for n in range(4)])
                out = lax.dot_general(
                    right, left, (((0,), (0,)), ((), ())), preferred_element_type=F32
                )
                if d > 0:
                    out += total[side]
                if d < 3:
                    total[side] = out
                else:
                    half = core if side == 0 else 1 - core
                    done = out.astype(BF16)
                    for n in range(4):
                        product[pl.ds(16 * half, 16), n] = done[
                            :, 128 * n : 128 * n + 128
                        ].reshape(16, 32, 128)

    def multiply1(panel, swap_b, swap_a, product):
        for d in range(4):
            at = (x + 4 - d) % 4
            pltpu.make_async_copy(panel.at[at], panel.at[at], recv_sems.at[1, at]).wait()
            copies = [
                swap(1, at, panel.at[at, :, 1], swap_b.at[at], 0),
                swap(1, at, panel.at[at, pl.ds(16 * (1 - core), 16), 0], swap_a.at[at], 1),
            ]
            for copy in copies:
                copy.start()
            for copy in copies:
                copy.wait()
            left = lanes(
                [
                    panel[at, pl.ds(16 * core, 16), 0].reshape(512, 128),
                    swap_a[at].reshape(512, 128),
                ]
            )
            for side in range(2):
                part = slice(16 * side, 16 * side + 16)
                right = lanes(
                    [panel[at, part, 1].reshape(512, 128), swap_b[at, part].reshape(512, 128)]
                )
                out = lax.dot_general(
                    right, left, (((1,), (1,)), ((), ())), preferred_element_type=F32
                )
                if d > 0:
                    out += total[side]
                if d < 3:
                    total[side] = out
                else:
                    done = out.astype(BF16)
                    for n in range(4):
                        product[part, n] = done[:, 128 * n : 128 * n + 128].reshape(16, 32, 128)

    def give_back(u, product, home):
        channel = (y * 32 + x * 8 if u == 0 else x * 32 + y * 8) + z_at

        def one(s, _):
            to = home_target(s)
            block = product.at[to[1], to[0] % 4]
            own = jnp.logical_and(s == 0, straight)

            @pl.when(own)
            def _():
                pltpu.make_async_copy(block, home.at[channel], back_recv.at[u]).start()

            @pl.when(jnp.logical_not(own))
            def _():
                pltpu.make_async_remote_copy(
                    block,
                    home.at[channel],
                    back_send.at[u],
                    back_recv.at[u],
                    device_id=to,
                    device_id_type=MESH,
                ).start()

            return 0

        lax.fori_loop(0, CHIPS, one, 0)

    def to_rows(source):
        def part(n, _):
            at = pl.multiple_of(n * 512, 512)
            rows32[pl.ds(at, 512), :] = source[pl.ds(n * 16, 16)].reshape(512, 128).astype(F32)
            return 0

        lax.fori_loop(0, 8, part, 0)

    def finish(u, n):
        t = lanes([take(n * 4 + q) for q in range(4)])
        tn = norm(t) * wide(gains[3 * u + 1]) + wide(gains[3 * u + 2])
        projected = jnp.dot(wt_out[u], tn.astype(BF16), preferred_element_type=F32)
        return (z[n].astype(F32) + projected * gate[n]).astype(BF16)

    def enter(u, n, block):
        z[n] = block
        x_all[n] = (norm(block.astype(F32)) * wide(gains[3 * u])).astype(BF16)

    weights(0)
    to_rows(pair)

    def first(n, _):
        enter(0, n, lanes([take(n * 4 + q).T for q in range(4)]).astype(BF16))
        return 0

    lax.fori_loop(0, BLOCKS, first, 0)
    forward(0, ab0, panel0)
    late_weights(0)
    gates(0)
    weights(1)
    late_weights(1)
    multiply0(panel0, swap_b0, product0)
    give_back(0, product0, home0)
    pltpu.make_async_copy(home0, home0, back_recv.at[0]).wait()
    to_rows(home0)

    def second(n, _):
        enter(1, n, finish(0, n))
        return 0

    lax.fori_loop(0, BLOCKS, second, 0)
    forward(1, ab1, panel1)
    gates(1)
    multiply1(panel1, swap_b1, swap_a1, product1)
    give_back(1, product1, home1)
    pltpu.make_async_copy(home1, home1, back_recv.at[1]).wait()
    to_rows(home1)

    def last(n, _):
        block = finish(1, n).astype(F32)
        for q in range(4):
            out_rows[pl.ds(n * 4 + q, 128, stride=32), :] = block[:, 128 * q : 128 * q + 128].T
        return 0

    lax.fori_loop(0, BLOCKS, last, 0)

    def leave(n, _):
        at = pl.multiple_of(n * 512, 512)
        updated[pl.ds(n * 16, 16)] = out_rows[pl.ds(at, 512), :].astype(BF16).reshape(16, 32, 128)
        return 0

    lax.fori_loop(0, 8, leave, 0)

    for u, ab in ((0, ab0), (1, ab1)):
        rest = ab.at[pl.ds(0, CHIPS - 1)]
        pltpu.make_async_copy(rest, rest, send_sems.at[u]).wait()
        rest = home0.at[pl.ds(0, CHIPS - 1)]
        pltpu.make_async_copy(rest, rest, back_send.at[u]).wait()

        @pl.when(jnp.logical_not(straight))
        def _(u=u, ab=ab):
            pltpu.make_async_copy(ab.at[0], ab.at[0], send_sems.at[u]).wait()
            pltpu.make_async_copy(home0.at[0], home0.at[0], back_send.at[u]).wait()


def local(pair, in_gain, w_in, out_gain, out_bias, w_out, w_gate_out):
    vmem = pl.BlockSpec(memory_space=pltpu.VMEM)
    spread = pltpu.VMEM((CHIPS, 2, 32, 128), BF16)
    block = pltpu.VMEM((CHIPS, 32, 128), BF16)
    return pl.pallas_call(
        kernel,
        out_shape=jax.ShapeDtypeStruct(pair.shape, BF16),
        in_specs=[vmem] * 7,
        out_specs=vmem,
        scratch_shapes=[
            pltpu.VMEM((4096, 128), F32),
            pltpu.VMEM((4096, 128), F32),
            pltpu.VMEM((BLOCKS, 128, WIDE), BF16),
            pltpu.VMEM((BLOCKS, 128, WIDE), BF16),
            pltpu.VMEM((BLOCKS, 128, WIDE), F32),
            pltpu.VMEM((2048, 128), F32),
            pltpu.VMEM((2, 512, 512), F32),
            pltpu.VMEM((6, 128, 128), F32),
            pltpu.VMEM((2, 4, 4, 32, 128), BF16),
            pltpu.VMEM((2, 128, 128), BF16),
            pltpu.VMEM((2, 128, 128), BF16),
            spread,
            spread,
            pltpu.VMEM((4, 8, 4, 2, 32, 128), BF16),
            pltpu.VMEM((4, 32, 2, 32, 128), BF16),
            pltpu.VMEM((4, 8, 4, 32, 128), BF16),
            pltpu.VMEM((4, 32, 32, 128), BF16),
            pltpu.VMEM((4, 16, 32, 128), BF16),
            pltpu.VMEM((32, 4, 32, 128), BF16),
            pltpu.VMEM((32, 4, 32, 128), BF16),
            block,
            block,
            pltpu.SemaphoreType.DMA((2,)),
            pltpu.SemaphoreType.DMA((2, 4)),
            pltpu.SemaphoreType.DMA((2, 2, 4)),
            pltpu.SemaphoreType.DMA((2, 2, 4)),
            pltpu.SemaphoreType.DMA((2,)),
            pltpu.SemaphoreType.DMA((2,)),
        ],
        compiler_params=pltpu.CompilerParams(
            collective_id=0, has_side_effects=True, vmem_limit_bytes=56 << 20
        ),
        name="triangles",
    )(pair, in_gain, w_in, out_gain, out_bias, w_out, w_gate_out)


def solution(mesh):
    in_specs = (P("row", "col", None), P(), P(), P(), P(), P(), P())
    out_specs = P("row", "col", None)
    return jax.shard_map(local, mesh=mesh, in_specs=in_specs, out_specs=out_specs, check_vma=False)
```

time: 537 us -> 191 us (0.36)
  waiting for transfers between devices: 294 us -> 0 us
  Pallas kernels: 0 us -> 188 us
  blocking collectives: 164 us -> 0 us
  starting transfers between devices: 23.4 us -> 0 us
  matrix products: 17.6 us -> 0 us
  local copies, waits for them, and re-layouts: 17.9 us -> 2.26 us
  between operations: 13.4 us -> 0.01 us
  other arithmetic: 6.21 us -> 0 us
    all_gather x3 -> x0, waiting for transfers between devices: 238 us -> none  [the longest x1 102 us: triangle(): left_piece = lax.all_gather(left_panel, 'row', axis=2, tiled=True)]
    pallas_call x0 -> x1, Pallas kernels: none -> 188 us  [local(): pl.pallas_call(kernel, out_shape=jax.ShapeDtypeStruct(pair.shape, BF16),...]
    all_to_all x4 -> x0, blocking collectives: 164 us -> none  [the longest x2 88.8 us: triangle(): lax.all_to_all(left, 'col', split_axis=0, concat_axis=1, tiled=True)]
    all_to_all x2 -> x0, waiting for transfers between devices: 56.6 us -> none  [triangle(): lax.all_to_all(product.astype(jnp.bfloat16), 'col', split_axis=1, concat_...]
    all_to_all x2 -> x0, starting transfers between devices: 23.1 us -> none  [triangle(): lax.all_to_all(product.astype(jnp.bfloat16), 'col', split_axis=1, concat_...]
    dot_general x8 -> x0, matrix products: 17.6 us -> none  [the longest x1 5.95 us: triangle(): jnp.einsum('cjk,cik->cji', right_piece, sliced, preferred_element_type=jn...]
    convert_element_type x9 -> x0, local copies, waits for them, and re-layouts: 11.2 us -> none  [the longest x2 3.56 us: triangle(): product.astype(jnp.bfloat16)]
  transfers between devices with their start and end apart: 5 -> 0, of which waited for: 5 -> 0; matrix products, arithmetic and copies ran while one was open for 1% -> 0% of each run, Pallas kernels for 0% -> 0%
where the time goes in v2:
time: 191 us; the launch traced here: 190 us
  Pallas kernels  188 us (98%)
  local copies, waits for them, and re-layouts  2.26 us (1%)
    pallas_call x1, Pallas kernels, local(): pl.pallas_call(kernel, out_shape=jax.ShapeDtypeStruct(pair.shape, BF16),...  188 us

profile of v2, /device:TPU:1, one launch (start us, length us, event | category | flops | bytes accessed | tf_op | source)
XLA Modules:
  0.0 190.5 jit_solution(1360279732743480442)
XLA Ops:
  0.0 188.2 %triangles.1 = bf16[128,32,128]{2,1,0:T(8,128)(2,1)} custom-call(bf16[128,32,128]{2,1,0:T(8,128)(2,1)} %pair.1, f32[2,128]{1,0:T(2,128)} %in_gain.1, bf16[2,128,512]{2,1,0:T(8,128)(2,1)} %w_in.1, f32[2,128]{1,0:T(2,128)} %out_gain.1, f32[2,128]{1,0:T(2,128)} %out_bias.1, bf16[2,128,128]{2,1,0:T(8,128)(2,1)} %w_out.1, bf16[2,128,128]{2,1,0:T(8,128)(2,1)} %w_gate.1), custom_call_target="tpu_custom_call" | custom-call | tf_op jit(solution)/shard_map/triangles/pallas_call | solution.py:344
  188.2 2.3 %copy.9 = bf16[128,32,128]{2,1,0:T(8,128)(2,1)} copy(bf16[128,32,128]{2,1,0:T(8,128)(2,1)} %triangles.1) | data formatting | bytes 2097152

commit v3 on v2

--- a/solution.py
+++ b/solution.py
@@ -42,7 +42,7 @@
     pair, in_gain, w_in, out_gain, out_bias, w_out, w_gate, updated,
     rows32, out_rows, z, x_all, gate, staged, total, gains, wt_in, wt_out, wt_gate,
     ab0, ab1, panel0, panel1, swap_b0, swap_b1, swap_a1, product0, product1, home0, home1,
-    send_sems, recv_sems, swap_send, swap_recv, back_send, back_recv,
+    send_sems, recv_sems, swap_send, swap_recv, back_send, back_recv, line_sems,
 ):
     bar = pltpu.get_barrier_semaphore()
     x, y, z_lo, z_hi, core = coordinates()
@@ -55,18 +55,19 @@
         to_x, to_y = (x + s // 32) % 4, (y + (s // 8) % 4) % 4
         return device(to_x, to_y, core, (z_hi + (s // 2) % 4) % 4, (core + s) % 2)
 
-    def greet(s, _):
-        @pl.when(jnp.logical_not(jnp.logical_and(s == 0, straight)))
-        def _():
-            pl.semaphore_signal(bar, inc=1, device_id=home_target(s), device_id_type=MESH)
-
-        return 0
-
-    lax.fori_loop(0, CHIPS, greet, 0)
-
-    @pl.when(jnp.logical_not(straight))
-    def _():
-        pl.semaphore_signal(bar, inc=1, device_id=partner, device_id_type=MESH)
+    along_z = [
+        device(x, y, (z_at + d) % 8 % 2, (z_at + d) % 8 // 2, other)
+        for d in range(8)
+        for other in (core, 1 - core)
+    ][1:]
+    along_y = [device(x, (y + d) % 4, z_lo, z_hi, core) for d in range(1, 4)]
+    along_x = [device((x + d) % 4, y, z_lo, z_hi, core) for d in range(1, 4)]
+
+    def greet(sem, devices):
+        for to in devices:
+            pl.semaphore_signal(sem, inc=1, device_id=to, device_id_type=MESH)
+
+    greet(bar, along_z + along_y + along_x)
 
     def flip(block):
         return block.astype(F32).T
@@ -125,7 +126,7 @@
             to_outer = (outer + d) % 4
             projections(u, ab, to_outer)
             if u == 0 and d == 0:
-                pl.semaphore_wait(bar, CHIPS)
+                pl.semaphore_wait(line_sems.at[1], 3)
 
             def spread(s, _, d=d, to_outer=to_outer):
                 to_inner, to_z = (inner + s // 8) % 4, (z_at + s) % 8
@@ -287,7 +288,12 @@
         enter(0, n, lanes([take(n * 4 + q).T for q in range(4)]).astype(BF16))
         return 0
 
-    lax.fori_loop(0, BLOCKS, first, 0)
+    pl.semaphore_wait(bar, 21)
+    greet(line_sems.at[0], along_y)
+    lax.fori_loop(0, 4, first, 0)
+    pl.semaphore_wait(line_sems.at[0], 3)
+    greet(line_sems.at[1], along_x)
+    lax.fori_loop(4, BLOCKS, first, 0)
     forward(0, ab0, panel0)
     late_weights(0)
     gates(0)
@@ -375,6 +381,7 @@
             pltpu.SemaphoreType.DMA((2, 2, 4)),
             pltpu.SemaphoreType.DMA((2,)),
             pltpu.SemaphoreType.DMA((2,)),
+            pltpu.SemaphoreType.REGULAR((2,)),
         ],
         compiler_params=pltpu.CompilerParams(
             collective_id=0, has_side_effects=True, vmem_limit_bytes=56 << 20

time: 191 us -> 189 us (0.990)
  no operation moved by 1% of the time
where the time goes in v3:
time: 189 us
  Pallas kernels  187 us (99%)
  local copies, waits for them, and re-layouts  2.26 us (1%)
    pallas_call x1, Pallas kernels, local(): pl.pallas_call(kernel, out_shape=jax.ShapeDtypeStruct(pair.shape, BF16),...  187 us

profile of v3, /device:TPU:1, one launch (start us, length us, event | category | flops | bytes accessed | tf_op | source)
XLA Modules:
  0.0 188.8 jit_solution(11353495414777802281)
XLA Ops:
  0.0 186.5 %triangles.1 = bf16[128,32,128]{2,1,0:T(8,128)(2,1)} custom-call(bf16[128,32,128]{2,1,0:T(8,128)(2,1)} %pair.1, f32[2,128]{1,0:T(2,128)} %in_gain.1, bf16[2,128,512]{2,1,0:T(8,128)(2,1)} %w_in.1, f32[2,128]{1,0:T(2,128)} %out_gain.1, f32[2,128]{1,0:T(2,128)} %out_bias.1, bf16[2,128,128]{2,1,0:T(8,128)(2,1)} %w_out.1, bf16[2,128,128]{2,1,0:T(8,128)(2,1)} %w_gate.1), custom_call_target="tpu_custom_call" | custom-call | tf_op jit(solution)/shard_map/triangles/pallas_call | solution.py:350
  186.5 2.3 %copy.9 = bf16[128,32,128]{2,1,0:T(8,128)(2,1)} copy(bf16[128,32,128]{2,1,0:T(8,128)(2,1)} %triangles.1) | data formatting | bytes 2097152

commit v4 on v2

v4 whole, which is shorter than its diff:
```python
import jax
import jax.numpy as jnp
from jax import lax
from jax.experimental import pallas as pl
from jax.experimental.pallas import tpu as pltpu
from jax.sharding import PartitionSpec as P

EPS = 1e-05
MESH = pl.DeviceIdType.MESH
CHIPS = 128
BLOCKS = 8
WIDE = 512

F32, BF16 = jnp.float32, jnp.bfloat16


def coordinates():
    row, col = lax.axis_index("row"), lax.axis_index("col")
    return row % 4, (col // 2) % 4, row // 4, col // 8, col % 2


def device(x, y, z_lo, z_hi, core):
    return z_lo * 4 + x, z_hi * 8 + y * 2 + core


def sigmoid(values):
    return 0.5 * jnp.tanh(0.5 * values) + 0.5


def norm(values):
    mean = jnp.sum(values, axis=0, keepdims=True) * (1.0 / 128)
    centred = values - mean
    var = jnp.sum(centred * centred, axis=0, keepdims=True) * (1.0 / 128)
    return centred * lax.rsqrt(var + EPS)


def wide(column):
    return jnp.concatenate([column] * (WIDE // 128), axis=1)


def kernel(
    pair, in_gain, w_in, out_gain, out_bias, w_out, w_gate, updated,
    pair_v, out_v, rows, out_rows, z, x_all, gate, staged, total, gains, wt_in, wt_out, wt_gate,
    ab0, ab1, panel0, panel1, swap_b0, swap_b1, swap_a1, product0, product1, home0, home1,
    send_sems, recv_sems, swap_send, swap_recv, back_send, back_recv, line_sem, local_sems,
):
    bar = pltpu.get_barrier_semaphore()
    x, y, z_lo, z_hi, core = coordinates()
    z_at = z_hi * 2 + z_lo
    col = lax.axis_index("col")
    partner = device(x, y, z_lo, z_hi, 1 - core)
    straight = core == z_lo
    parity = (x + y) % 2

    along_y = [device(x, (y + d) % 4, z_lo, z_hi, core) for d in range(1, 4)]

    def greet(sem, to):
        pl.semaphore_signal(sem, inc=1, device_id=to, device_id_type=MESH)

    def greet_plane(s, _):
        @pl.when(jnp.logical_not(jnp.logical_and(s == 0, straight)))
        def _():
            greet(bar, device((x + s // 8) % 4, y, core, (z_hi + s // 2) % 4, (core + s) % 2))

        return 0

    lax.fori_loop(0, 32, greet_plane, 0)
    for to in along_y:
        greet(bar, to)

    @pl.when(jnp.logical_not(straight))
    def _():
        greet(bar, partner)

    def half_of(ref, h):
        return ref.at[:, pl.ds(16 * h, 16)]

    arrivals = [
        pltpu.make_async_copy(half_of(pair, h), half_of(pair_v, h), local_sems.at[h])
        for h in range(2)
    ]
    for copy in arrivals:
        copy.start()

    def flip(block):
        return block.astype(F32).T

    def weights(u):
        for kind in range(4):
            turned = flip(w_in[u, :, 128 * kind : 128 * kind + 128]).astype(BF16)
            wt_in[u, :, kind] = turned.reshape(4, 32, 128)
        gains[3 * u] = jnp.broadcast_to(in_gain[u : u + 1, :], (128, 128)).T

    def late_weights(u):
        wt_out[u] = flip(w_out[u]).astype(BF16)
        wt_gate[u] = flip(w_gate[u]).astype(BF16)
        gains[3 * u + 1] = jnp.broadcast_to(out_gain[u : u + 1, :], (128, 128)).T
        gains[3 * u + 2] = jnp.broadcast_to(out_bias[u : u + 1, :], (128, 128)).T

    def take(t):
        return rows[pl.ds(t, 128, stride=16), :]

    def to_rows(source):
        def part(n, _):
            at = pl.multiple_of(n * 512, 512)
            rows[pl.ds(at, 512), :] = source[pl.ds(n * 32, 32)].reshape(512, 128).astype(F32)
            return 0

        lax.fori_loop(0, 4, part, 0)

    def projections(u, h, ab, group):
        lhs = wt_in[u, group].reshape(128, 128)

        def block(n, _):
            mixed = jnp.dot(lhs, x_all[4 * h + n], preferred_element_type=F32)
            gated = mixed[0:64] * sigmoid(mixed[64:128])
            for kind in range(2):
                for q in range(4):
                    staged[pl.ds(kind * 16 + n * 4 + q, 32, stride=32), :] = gated[
                        32 * kind : 32 * kind + 32, 128 * q : 128 * q + 128
                    ]
            return 0

        lax.fori_loop(0, 4, block, 0)

        def pack(d, _):
            at = pl.multiple_of(d * 256, 256)
            ab[h, pl.ds(group * 32 + d * 8, 8)] = (
                staged[pl.ds(at, 256), :].astype(BF16).reshape(8, 2, 16, 128)
            )
            return 0

        lax.fori_loop(0, 4, pack, 0)

    def gates(u):
        def block(n, _):
            gate[n] = sigmoid(jnp.dot(wt_gate[u], x_all[n], preferred_element_type=F32))
            return 0

        lax.fori_loop(0, BLOCKS, block, 0)

    def near(at):
        return [at, at + 1 - 2 * (at % 2), (at + 2) % 4, 3 - at]

    def forward(u, h, ab, panel):
        outer, inner = (y, x) if u == 0 else (x, y)
        slot = panel.at[y, z_hi * 2 + core, x, h] if u == 0 else panel.at[x, col, h]
        send, recv = send_sems.at[u], recv_sems.at[u, h, outer]
        for side in range(2):
            for e in range(4):
                to_outer = near(outer)[e]
                if e % 2 == 0:
                    projections(u, h, ab, side * 2 + to_outer // 2)
                if u == 0 and h == 0 and side == 0 and e == 0:
                    pl.semaphore_wait(bar, 35)
                    for to in along_y:
                        greet(line_sem, to)
                if u == 0 and h == 0 and side == 0 and e == 1:
                    pl.semaphore_wait(line_sem, 3)

                def spread(s, _, to_outer=to_outer, side=side, e=e):
                    odd = (side + to_outer) % 2
                    to_inner = odd + 2 * ((inner // 2 + s // 8) % 2)
                    to_z = (z_at + s) % 8
                    channel = side * 64 + to_outer * 16 + (to_inner // 2) * 8 + to_z
                    to_x, to_y = (to_inner, to_outer) if u == 0 else (to_outer, to_inner)

                    def remote():
                        pltpu.make_async_remote_copy(
                            ab.at[h, channel],
                            slot,
                            send,
                            recv,
                            device_id=device(to_x, to_y, to_z % 2, to_z // 2, z_lo),
                            device_id_type=MESH,
                        ).start()

                    if e > 0:
                        remote()
                    else:
                        own = jnp.logical_and(jnp.logical_and(s == 0, parity == side), straight)

                        @pl.when(own)
                        def _():
                            pltpu.make_async_copy(ab.at[h, channel], slot, recv).start()

                        @pl.when(jnp.logical_not(own))
                        def _():
                            remote()

                    return 0

                lax.fori_loop(0, 16, spread, 0)

    def swap(u, chunk, source, target, at):
        return pltpu.make_async_remote_copy(
            source,
            target,
            swap_send.at[u, at, chunk],
            swap_recv.at[u, at, chunk],
            device_id=partner,
            device_id_type=MESH,
        )

    def lanes(parts):
        return jnp.concatenate(parts, axis=1)

    def keep(product, part, out):
        done = out.astype(BF16)
        for n in range(4):
            product[part, n] = done[:, 128 * n : 128 * n + 128].reshape(16, 2, 16, 128)

    def multiply0(panel, swap_b, product):
        for d, at in enumerate(near(y)):
            for h in range(2):
                part = panel.at[at, :, :, h]
                pltpu.make_async_copy(part, part, recv_sems.at[0, h, at]).wait()
            copy = swap(0, at, panel.at[at, :, :, :, 1], swap_b.at[at], 0)
            copy.start()
            left = lanes([panel[at, :, n, :, 0].reshape(256, 128) for n in range(4)])
            for side in range(2):
                if side == 0:
                    right = lanes([panel[at, :, n, :, 1].reshape(256, 128) for n in range(4)])
                else:
                    copy.wait()
                    right = lanes([swap_b[at, :, n].reshape(256, 128) for n in range(4)])
                out = lax.dot_general(
                    right, left, (((0,), (0,)), ((), ())), preferred_element_type=F32
                )
                if d > 0:
                    out += total[side]
                if d < 3:
                    total[side] = out
                else:
                    keep(product, pl.ds(16 * (core if side == 0 else 1 - core), 16), out)

    def multiply1(panel, swap_b, swap_a, product):
        for d, at in enumerate(near(x)):
            for h in range(2):
                part = panel.at[at, :, h]
                pltpu.make_async_copy(part, part, recv_sems.at[1, h, at]).wait()
            copies = [
                swap(1, at, panel.at[at, :, :, 1], swap_b.at[at], 0),
                swap(1, at, panel.at[at, pl.ds(16 * (1 - core), 16), :, 0], swap_a.at[at], 1),
            ]
            for copy in copies:
                copy.start()
            for copy in copies:
                copy.wait()
            left = lanes(
                [
                    panel[at, pl.ds(16 * core, 16), :, 0].reshape(512, 128),
                    swap_a[at].reshape(512, 128),
                ]
            )
            for side in range(2):
                part = slice(16 * side, 16 * side + 16)
                right = lanes(
                    [panel[at, part, :, 1].reshape(512, 128), swap_b[at, part].reshape(512, 128)]
                )
                out = lax.dot_general(
                    right, left, (((1,), (1,)), ((), ())), preferred_element_type=F32
                )
                if d > 0:
                    out += total[side]
                if d < 3:
                    total[side] = out
                else:
                    keep(product, part, out)

    def home_target(s):
        to_x, to_y = (x + s // 32) % 4, (y + (s // 8) % 4) % 4
        return device(to_x, to_y, core, (z_hi + (s // 2) % 4) % 4, (core + s) % 2)

    def give_back(u, product, home):
        outer, inner = (y, x) if u == 0 else (x, y)
        channel = parity * 64 + outer * 16 + (inner // 2) * 8 + z_at
        for h in range(2):

            def one(s, _, h=h):
                to = home_target(s)
                block, slot = product.at[to[1], to[0] % 4, h], home.at[h, channel]
                own = jnp.logical_and(s == 0, straight)

                @pl.when(own)
                def _():
                    pltpu.make_async_copy(block, slot, back_recv.at[u, h]).start()

                @pl.when(jnp.logical_not(own))
                def _():
                    pltpu.make_async_remote_copy(
                        block,
                        slot,
                        back_send.at[u],
                        back_recv.at[u, h],
                        device_id=to,
                        device_id_type=MESH,
                    ).start()

                return 0

            lax.fori_loop(0, CHIPS, one, 0)

    def received(u, h, home):
        pltpu.make_async_copy(home.at[h], home.at[h], back_recv.at[u, h]).wait()
        to_rows(home.at[h])

    def finish(u, h, n):
        t = lanes([take(n * 4 + q) for q in range(4)])
        tn = norm(t) * wide(gains[3 * u + 1]) + wide(gains[3 * u + 2])
        projected = jnp.dot(wt_out[u], tn.astype(BF16), preferred_element_type=F32)
        return (z[4 * h + n].astype(F32) + projected * gate[4 * h + n]).astype(BF16)

    def enter(u, h, n, block):
        z[4 * h + n] = block
        x_all[4 * h + n] = (norm(block.astype(F32)) * wide(gains[3 * u])).astype(BF16)

    weights(0)
    for h in range(2):
        arrivals[h].wait()
        to_rows(half_of(pair_v, h))

        def first(n, _, h=h):
            enter(0, h, n, lanes([take(n * 4 + q).T for q in range(4)]).astype(BF16))
            return 0

        lax.fori_loop(0, 4, first, 0)
        forward(0, h, ab0, panel0)
    late_weights(0)
    gates(0)
    weights(1)
    late_weights(1)
    multiply0(panel0, swap_b0, product0)
    give_back(0, product0, home0)
    for h in range(2):
        received(0, h, home0)

        def second(n, _, h=h):
            enter(1, h, n, finish(0, h, n))
            return 0

        lax.fori_loop(0, 4, second, 0)
        forward(1, h, ab1, panel1)
    gates(1)
    multiply1(panel1, swap_b1, swap_a1, product1)
    give_back(1, product1, home1)
    leaving = []
    for h in range(2):
        received(1, h, home1)

        def last(n, _, h=h):
            block = finish(1, h, n).astype(F32)
            for q in range(4):
                staged_out = block[:, 128 * q : 128 * q + 128].T
                out_rows[pl.ds(n * 4 + q, 128, stride=16), :] = staged_out
            return 0

        lax.fori_loop(0, 4, last, 0)

        def leave(n, _, h=h):
            at = pl.multiple_of(n * 512, 512)
            out_v[pl.ds(n * 32, 32), 16 * h : 16 * h + 16] = (
                out_rows[pl.ds(at, 512), :].astype(BF16).reshape(32, 16, 128)
            )
            return 0

        lax.fori_loop(0, 4, leave, 0)
        copy = pltpu.make_async_copy(half_of(out_v, h), half_of(updated, h), local_sems.at[2 + h])
        copy.start()
        leaving.append(copy)

    for u, ab in ((0, ab0), (1, ab1)):
        for sent, sem in ((ab, send_sems.at[u]), (home0, back_send.at[u])):
            rest = sent.at[:, pl.ds(0, CHIPS - 1)]
            pltpu.make_async_copy(rest, rest, sem).wait()

            @pl.when(jnp.logical_not(straight))
            def _(sent=sent, sem=sem):
                rest = sent.at[:, 0]
                pltpu.make_async_copy(rest, rest, sem).wait()

    for copy in leaving:
        copy.wait()


def local(pair, in_gain, w_in, out_gain, out_bias, w_out, w_gate_out):
    vmem = pl.BlockSpec(memory_space=pltpu.VMEM)
    anywhere = pl.BlockSpec(memory_space=pl.ANY)
    spread = pltpu.VMEM((2, CHIPS, 2, 16, 128), BF16)
    block = pltpu.VMEM((2, CHIPS, 16, 128), BF16)
    whole = pltpu.VMEM((128, 32, 128), BF16)
    return pl.pallas_call(
        kernel,
        out_shape=jax.ShapeDtypeStruct(pair.shape, BF16),
        in_specs=[anywhere] + [vmem] * 6,
        out_specs=anywhere,
        scratch_shapes=[
            whole,
            whole,
            pltpu.VMEM((2048, 128), F32),
            pltpu.VMEM((2048, 128), F32),
            pltpu.VMEM((BLOCKS, 128, WIDE), BF16),
            pltpu.VMEM((BLOCKS, 128, WIDE), BF16),
            pltpu.VMEM((BLOCKS, 128, WIDE), F32),
            pltpu.VMEM((1024, 128), F32),
            pltpu.VMEM((2, 512, 512), F32),
            pltpu.VMEM((6, 128, 128), F32),
            pltpu.VMEM((2, 4, 4, 32, 128), BF16),
            pltpu.VMEM((2, 128, 128), BF16),
            pltpu.VMEM((2, 128, 128), BF16),
            spread,
            spread,
            pltpu.VMEM((4, 8, 4, 2, 2, 16, 128), BF16),
            pltpu.VMEM((4, 32, 2, 2, 16, 128), BF16),
            pltpu.VMEM((4, 8, 4, 2, 16, 128), BF16),
            pltpu.VMEM((4, 32, 2, 16, 128), BF16),
            pltpu.VMEM((4, 16, 2, 16, 128), BF16),
            pltpu.VMEM((32, 4, 2, 16, 128), BF16),
            pltpu.VMEM((32, 4, 2, 16, 128), BF16),
            block,
            block,
            pltpu.SemaphoreType.DMA((2,)),
            pltpu.SemaphoreType.DMA((2, 2, 4)),
            pltpu.SemaphoreType.DMA((2, 2, 4)),
            pltpu.SemaphoreType.DMA((2, 2, 4)),
            pltpu.SemaphoreType.DMA((2,)),
            pltpu.SemaphoreType.DMA((2, 2)),
            pltpu.SemaphoreType.REGULAR,
            pltpu.SemaphoreType.DMA((4,)),
        ],
        compiler_params=pltpu.CompilerParams(
            collective_id=0, has_side_effects=True, vmem_limit_bytes=56 << 20
        ),
        name="triangles",
    )(pair, in_gain, w_in, out_gain, out_bias, w_out, w_gate_out)


def solution(mesh):
    in_specs = (P("row", "col", None), P(), P(), P(), P(), P(), P())
    out_specs = P("row", "col", None)
    return jax.shard_map(local, mesh=mesh, in_specs=in_specs, out_specs=out_specs, check_vma=False)
```

time: 191 us -> 176 us (0.921)
  Pallas kernels: 188 us -> 173 us
    pallas_call x1, Pallas kernels: 188 us -> 173 us  [local(): pl.pallas_call(kernel, out_shape=jax.ShapeDtypeStruct(pair.shape, BF16),...]
where the time goes in v4:
time: 176 us
  Pallas kernels  173 us (98%)
  local copies, waits for them, and re-layouts  2.26 us (1%)
    pallas_call x1, Pallas kernels, local(): pl.pallas_call(kernel, out_shape=jax.ShapeDtypeStruct(pair.shape, BF16),...  173 us

profile of v4, /device:TPU:1, one launch (start us, length us, event | category | flops | bytes accessed | tf_op | source)
XLA Modules:
  0.0 175.7 jit_solution(6073862753655491454)
XLA Ops:
  0.0 173.4 %triangles.1 = bf16[128,32,128]{2,1,0:T(8,128)(2,1)} custom-call(bf16[128,32,128]{2,1,0:T(8,128)(2,1)} %pair.1, f32[2,128]{1,0:T(2,128)} %in_gain.1, bf16[2,128,512]{2,1,0:T(8,128)(2,1)} %w_in.1, f32[2,128]{1,0:T(2,128)} %out_gain.1, f32[2,128]{1,0:T(2,128)} %out_bias.1, bf16[2,128,128]{2,1,0:T(8,128)(2,1)} %w_out.1, bf16[2,128,128]{2,1,0:T(8,128)(2,1)} %w_gate.1), custom_call_target="tpu_custom_call" | custom-call | tf_op jit(solution)/shard_map/triangles/pallas_call | solution.py:392
  173.4 2.3 %copy.9 = bf16[128,32,128]{2,1,0:T(8,128)(2,1)} copy(bf16[128,32,128]{2,1,0:T(8,128)(2,1)} %triangles.1) | data formatting | bytes 2097152

commit v5 on v4

v5 whole, which is shorter than its diff:
```python
import jax
import jax.numpy as jnp
from jax import lax
from jax.experimental import pallas as pl
from jax.experimental.pallas import tpu as pltpu
from jax.sharding import PartitionSpec as P

EPS = 1e-05
MESH = pl.DeviceIdType.MESH
CHIPS = 128
BLOCKS = 8
WIDE = 512

F32, BF16 = jnp.float32, jnp.bfloat16


def coordinates():
    row, col = lax.axis_index("row"), lax.axis_index("col")
    return row % 4, (col // 2) % 4, row // 4, col // 8, col % 2


def device(x, y, z_lo, z_hi, core):
    return z_lo * 4 + x, z_hi * 8 + y * 2 + core


def sigmoid(values):
    return 0.5 * jnp.tanh(0.5 * values) + 0.5


def norm(values):
    mean = jnp.sum(values, axis=0, keepdims=True) * (1.0 / 128)
    centred = values - mean
    var = jnp.sum(centred * centred, axis=0, keepdims=True) * (1.0 / 128)
    return centred * lax.rsqrt(var + EPS)


def wide(column):
    return jnp.concatenate([column] * (WIDE // 128), axis=1)


def kernel(
    pair, in_gain, w_in, out_gain, out_bias, w_out, w_gate, updated,
    pair_v, out_v, rows, out_rows, z, x_all, gate, staged, gains, wt_in, wt_out, wt_gate,
    ab0, ab1, panel0, panel1, swap_b0, swap_b1, swap_a1, product0, product1, home0, home1,
    send_sems, recv_sems, swap_send, swap_recv, back_send, back_recv, line_sems, local_sems,
):
    bar = pltpu.get_barrier_semaphore()
    x, y, z_lo, z_hi, core = coordinates()
    z_at = z_hi * 2 + z_lo
    col = lax.axis_index("col")
    partner = device(x, y, z_lo, z_hi, 1 - core)
    straight = core == z_lo

    along_y = [device(x, (y + d) % 4, z_lo, z_hi, core) for d in range(1, 4)]
    along_x = [device((x + d) % 4, y, z_lo, z_hi, core) for d in range(1, 4)]

    def greet(sem, devices):
        for to in devices:
            pl.semaphore_signal(sem, inc=1, device_id=to, device_id_type=MESH)

    column = [device(x, y, core, (z_hi + n // 2) % 4, (core + n) % 2) for n in range(8)]
    greet(bar, column[1:])

    @pl.when(straight)
    def _():
        greet(bar, along_y + along_x)

    @pl.when(jnp.logical_not(straight))
    def _():
        greet(bar, along_y + along_x + [column[0], partner])

    def half_of(ref, h):
        return ref.at[:, pl.ds(16 * h, 16)]

    arrival = pltpu.make_async_copy(pair, pair_v, local_sems.at[0])
    arrival.start()

    def flip(block):
        return block.astype(F32).T

    def weights(u):
        for kind in range(4):
            turned = flip(w_in[u, :, 128 * kind : 128 * kind + 128]).astype(BF16)
            wt_in[u, :, kind] = turned.reshape(4, 32, 128)
        gains[3 * u] = jnp.broadcast_to(in_gain[u : u + 1, :], (128, 128)).T

    def late_weights(u):
        wt_out[u] = flip(w_out[u]).astype(BF16)
        wt_gate[u] = flip(w_gate[u]).astype(BF16)
        gains[3 * u + 1] = jnp.broadcast_to(out_gain[u : u + 1, :], (128, 128)).T
        gains[3 * u + 2] = jnp.broadcast_to(out_bias[u : u + 1, :], (128, 128)).T

    def take(t, tokens):
        return rows[pl.ds(t, 128, stride=tokens), :]

    def to_rows(source):
        tokens = source.shape[1]
        some = 512 // tokens

        def part(n, _):
            at = pl.multiple_of(n * 512, 512)
            rows[pl.ds(at, 512), :] = source[pl.ds(n * some, some)].reshape(512, 128).astype(F32)
            return 0

        lax.fori_loop(0, 128 // some, part, 0)

    def projections(u, h, ab, group):
        lhs = wt_in[u, group].reshape(128, 128)
        tokens = ab.shape[2]

        def block(n, _):
            mixed = jnp.dot(lhs, x_all[4 * h + n], preferred_element_type=F32)
            gated = mixed[0:64] * sigmoid(mixed[64:128])
            for kind in range(2):
                for q in range(4):
                    staged[pl.ds(kind * tokens + n * 4 + q, 32, stride=2 * tokens), :] = gated[
                        32 * kind : 32 * kind + 32, 128 * q : 128 * q + 128
                    ]
            return 0

        lax.fori_loop(0, tokens // 4, block, 0)
        some = 128 // tokens

        def pack(d, _):
            at = pl.multiple_of(d * 256, 256)
            ab[pl.ds(group * 32 + d * some, some)] = (
                staged[pl.ds(at, 256), :].astype(BF16).reshape(some, 2, tokens, 128)
            )
            return 0

        lax.fori_loop(0, 32 // some, pack, 0)

    def gates(u):
        def block(n, _):
            gate[n] = sigmoid(jnp.dot(wt_gate[u], x_all[n], preferred_element_type=F32))
            return 0

        lax.fori_loop(0, BLOCKS, block, 0)

    def near(u):
        if u == 0:
            return [(x + d) % 4 for d in (0, 2, 1, 3)]
        return [y, y + 1 - 2 * (y % 2), (y + 2) % 4, 3 - y]

    def forward(u, h, ab, slot, recv):
        inner = y if u == 0 else x
        send = send_sems.at[u]
        for e, to_outer in enumerate(near(u)):
            projections(u, h, ab, to_outer)
            if u == 0 and e == 0:
                pl.semaphore_wait(bar, 14)
                greet(line_sems.at[0], along_y)
            if u == 0 and e == 1:
                pl.semaphore_wait(line_sems.at[1], 3)

            def spread(s, _, to_outer=to_outer, e=e):
                to_inner, to_z = (inner + s // 8) % 4, (z_at + s) % 8
                channel = to_outer * 32 + to_inner * 8 + to_z
                to_x, to_y = (to_outer, to_inner) if u == 0 else (to_inner, to_outer)

                def remote():
                    pltpu.make_async_remote_copy(
                        ab.at[channel],
                        slot,
                        send,
                        recv,
                        device_id=device(to_x, to_y, to_z % 2, to_z // 2, z_lo),
                        device_id_type=MESH,
                    ).start()

                if e > 0:
                    remote()
                else:
                    own = jnp.logical_and(s == 0, straight)

                    @pl.when(own)
                    def _():
                        pltpu.make_async_copy(ab.at[channel], slot, recv).start()

                    @pl.when(jnp.logical_not(own))
                    def _():
                        remote()

                return 0

            if u == 0 and e == 0:
                lax.fori_loop(0, 8, spread, 0)
                pl.semaphore_wait(line_sems.at[0], 3)
                greet(line_sems.at[1], along_x)
                lax.fori_loop(8, 32, spread, 0)
            else:
                lax.fori_loop(0, 32, spread, 0)

    def swap(u, chunk, source, target, at):
        return pltpu.make_async_remote_copy(
            source,
            target,
            swap_send.at[u, at, chunk],
            swap_recv.at[u, at, chunk],
            device_id=partner,
            device_id_type=MESH,
        )

    def lanes(parts):
        return jnp.concatenate(parts, axis=1)

    def product_of(right, left, over):
        return lax.dot_general(
            right, left, (((over,), (over,)), ((), ())), preferred_element_type=F32
        ).astype(BF16)

    def multiply0(panel, swap_b, product, home):
        def left(p):
            return lanes([panel[p + 2 * n, :, 0].reshape(1024, 128) for n in range(2)])

        def right(p, side):
            if side == 0:
                return lanes([panel[p + 2 * n, :, 1].reshape(1024, 128) for n in range(2)])
            return lanes([swap_b[p + 2 * n].reshape(1024, 128) for n in range(2)])

        def part(p, q, side):
            out = product_of(right(p, side), left(q), 0)
            half = core if side == 0 else 1 - core
            for n in range(2):
                for m in range(2):
                    product[pl.ds(16 * half + 4 * (p + 2 * n), 4), q + 2 * m] = out[
                        128 * n : 128 * n + 128, 128 * m : 128 * m + 128
                    ].reshape(4, 2, 16, 128)

        def arrive(at):
            pltpu.make_async_copy(panel.at[at], panel.at[at], recv_sems.at[at]).wait()
            copy = swap(0, at, panel.at[at, :, 1], swap_b.at[at], 0)
            copy.start()
            return copy

        p = x % 2
        order = near(0)
        copies = [arrive(at) for at in order[:2]]
        part(p, p, 0)
        for copy in copies:
            copy.wait()
        part(p, p, 1)
        give_back(0, p, product, home, ((0, 0),), (0, 1))
        copies = [arrive(at) for at in order[2:]]
        for side in range(2):
            if side == 1:
                for copy in copies:
                    copy.wait()
            part(p, 1 - p, side)
            part(1 - p, p, side)
            part(1 - p, 1 - p, side)
        for h in range(2):
            give_back(0, p, product, home, ((0, 1), (1, 0), (1, 1)), (h,))

    def multiply1(panel, swap_b, swap_a, product, home):
        def left(p):
            def some(source, start):
                return jnp.concatenate(
                    [
                        source(2 * p + m, pl.ds(start + 2 * n, 2)).reshape(64, 128)
                        for n in range(2)
                        for m in range(2)
                    ],
                    axis=0,
                )

            return lanes(
                [some(lambda at, zc: panel[at, zc, n, :, 0], 4 * core) for n in range(4)]
                + [some(lambda at, zc: swap_a[at, zc, n], 0) for n in range(4)]
            )

        def right(at):
            return lanes(
                [panel[at, :, n, :, 1].reshape(256, 128) for n in range(4)]
                + [swap_b[at, :, n].reshape(256, 128) for n in range(4)]
            )

        def part(p, q):
            for m in range(2):
                out = product_of(right(2 * p + m), left(q), 1)
                for n in range(2):
                    product[2 * p + m, :, 2 * n + q] = out[:, 128 * n : 128 * n + 128].reshape(
                        8, 2, 16, 128
                    )

        def arrive(at):
            for h in range(2):
                block = panel.at[at, :, :, h]
                pltpu.make_async_copy(block, block, recv_sems.at[4 + 4 * h + at]).wait()
            copies = [
                swap(1, at, panel.at[at, :, :, :, 1], swap_b.at[at], 0),
                swap(1, at, panel.at[at, pl.ds(4 * (1 - core), 4), :, :, 0], swap_a.at[at], 1),
            ]
            for copy in copies:
                copy.start()
            return copies

        p = y // 2
        order = near(1)
        for copy in arrive(order[0]) + arrive(order[1]):
            copy.wait()
        part(p, p)
        give_back(1, p, product, home, ((0, 0),), (0, 1))
        for copy in arrive(order[2]) + arrive(order[3]):
            copy.wait()
        part(p, 1 - p)
        part(1 - p, p)
        part(1 - p, 1 - p)
        for h in range(2):
            give_back(1, p, product, home, ((0, 1), (1, 0), (1, 1)), (h,))

    def give_back(u, p, product, home, quarters, halves):
        channel = (x * 32 + y * 8 if u == 0 else y * 32 + x * 8) + z_at
        for h in halves:
            for of_x, of_y in quarters:

                def one(s, _, h=h, of_x=of_x, of_y=of_y):
                    to_x = (p + of_x) % 2 + 2 * ((x // 2 + s // 16) % 2)
                    to_y = 2 * ((p + of_y) % 2) + (y + s // 8) % 2
                    to_z, to_core = (z_hi + s // 2) % 4, (core + s) % 2
                    to = device(to_x, to_y, core, to_z, to_core)
                    if u == 0:
                        block = product.at[to[1], to_x, h]
                    else:
                        block = product.at[to_y, to_z * 2 + to_core, to_x, h]
                    slot = home.at[h, channel]
                    here = jnp.logical_and(to_x == x, to_y == y)
                    own = jnp.logical_and(jnp.logical_and(s % 8 == 0, straight), here)

                    @pl.when(own)
                    def _():
                        pltpu.make_async_copy(block, slot, back_recv.at[u, h]).start()

                    @pl.when(jnp.logical_not(own))
                    def _():
                        pltpu.make_async_remote_copy(
                            block,
                            slot,
                            back_send.at[u],
                            back_recv.at[u, h],
                            device_id=to,
                            device_id_type=MESH,
                        ).start()

                    return 0

                lax.fori_loop(0, 32, one, 0)

    def received(u, h, home):
        pltpu.make_async_copy(home.at[h], home.at[h], back_recv.at[u, h]).wait()
        to_rows(home.at[h])

    def finish(u, h, n):
        t = lanes([take(n * 4 + q, 16) for q in range(4)])
        tn = norm(t) * wide(gains[3 * u + 1]) + wide(gains[3 * u + 2])
        projected = jnp.dot(wt_out[u], tn.astype(BF16), preferred_element_type=F32)
        return (z[4 * h + n].astype(F32) + projected * gate[4 * h + n]).astype(BF16)

    def enter(u, h, n, block):
        z[4 * h + n] = block
        x_all[4 * h + n] = (norm(block.astype(F32)) * wide(gains[3 * u])).astype(BF16)

    weights(0)
    arrival.wait()
    to_rows(pair_v)

    def first(n, _):
        enter(0, 0, n, lanes([take(n * 4 + q, 32).T for q in range(4)]).astype(BF16))
        return 0

    lax.fori_loop(0, BLOCKS, first, 0)
    forward(0, 0, ab0, panel0.at[x, col], recv_sems.at[x])
    late_weights(0)
    gates(0)
    weights(1)
    late_weights(1)
    multiply0(panel0, swap_b0, product0, home0)
    for h in range(2):
        received(0, h, home0)

        def second(n, _, h=h):
            enter(1, h, n, finish(0, h, n))
            return 0

        lax.fori_loop(0, 4, second, 0)
        slot = panel1.at[y, z_hi * 2 + core, x, h]
        forward(1, h, ab1.at[h], slot, recv_sems.at[4 + 4 * h + y])
    gates(1)
    multiply1(panel1, swap_b1, swap_a1, product1, home1)
    leaving = []
    for h in range(2):
        received(1, h, home1)

        def last(n, _, h=h):
            block = finish(1, h, n).astype(F32)
            for q in range(4):
                staged_out = block[:, 128 * q : 128 * q + 128].T
                out_rows[pl.ds(n * 4 + q, 128, stride=16), :] = staged_out
            return 0

        lax.fori_loop(0, 4, last, 0)

        def leave(n, _, h=h):
            at = pl.multiple_of(n * 512, 512)
            out_v[pl.ds(n * 32, 32), 16 * h : 16 * h + 16] = (
                out_rows[pl.ds(at, 512), :].astype(BF16).reshape(32, 16, 128)
            )
            return 0

        lax.fori_loop(0, 4, leave, 0)
        copy = pltpu.make_async_copy(half_of(out_v, h), half_of(updated, h), local_sems.at[1 + h])
        copy.start()
        leaving.append(copy)

    for sent, sem in (
        (ab0, send_sems.at[0]),
        (ab1, send_sems.at[1]),
        (home0, back_send.at[0]),
        (home1, back_send.at[1]),
    ):
        chips = () if sent is ab0 else (slice(None),)
        rest = sent.at[(*chips, pl.ds(0, CHIPS - 1))]
        pltpu.make_async_copy(rest, rest, sem).wait()

        @pl.when(jnp.logical_not(straight))
        def _(sent=sent, sem=sem, chips=chips):
            rest = sent.at[(*chips, 0)]
            pltpu.make_async_copy(rest, rest, sem).wait()

    for copy in leaving:
        copy.wait()


def local(pair, in_gain, w_in, out_gain, out_bias, w_out, w_gate_out):
    vmem = pl.BlockSpec(memory_space=pltpu.VMEM)
    anywhere = pl.BlockSpec(memory_space=pl.ANY)
    block = pltpu.VMEM((2, CHIPS, 16, 128), BF16)
    whole = pltpu.VMEM((128, 32, 128), BF16)
    return pl.pallas_call(
        kernel,
        out_shape=jax.ShapeDtypeStruct(pair.shape, BF16),
        in_specs=[anywhere] + [vmem] * 6,
        out_specs=anywhere,
        scratch_shapes=[
            whole,
            whole,
            pltpu.VMEM((4096, 128), F32),
            pltpu.VMEM((2048, 128), F32),
            pltpu.VMEM((BLOCKS, 128, WIDE), BF16),
            pltpu.VMEM((BLOCKS, 128, WIDE), BF16),
            pltpu.VMEM((BLOCKS, 128, WIDE), F32),
            pltpu.VMEM((2048, 128), F32),
            pltpu.VMEM((6, 128, 128), F32),
            pltpu.VMEM((2, 4, 4, 32, 128), BF16),
            pltpu.VMEM((2, 128, 128), BF16),
            pltpu.VMEM((2, 128, 128), BF16),
            pltpu.VMEM((CHIPS, 2, 32, 128), BF16),
            pltpu.VMEM((2, CHIPS, 2, 16, 128), BF16),
            pltpu.VMEM((4, 32, 2, 32, 128), BF16),
            pltpu.VMEM((4, 8, 4, 2, 2, 16, 128), BF16),
            pltpu.VMEM((4, 32, 32, 128), BF16),
            pltpu.VMEM((4, 8, 4, 2, 16, 128), BF16),
            pltpu.VMEM((4, 4, 4, 2, 16, 128), BF16),
            pltpu.VMEM((32, 4, 2, 16, 128), BF16),
            pltpu.VMEM((4, 8, 4, 2, 16, 128), BF16),
            block,
            block,
            pltpu.SemaphoreType.DMA((2,)),
            pltpu.SemaphoreType.DMA((12,)),
            pltpu.SemaphoreType.DMA((2, 2, 4)),
            pltpu.SemaphoreType.DMA((2, 2, 4)),
            pltpu.SemaphoreType.DMA((2,)),
            pltpu.SemaphoreType.DMA((2, 2)),
            pltpu.SemaphoreType.REGULAR((2,)),
            pltpu.SemaphoreType.DMA((3,)),
        ],
        compiler_params=pltpu.CompilerParams(
            collective_id=0, has_side_effects=True, vmem_limit_bytes=56 << 20
        ),
        name="triangles",
    )(pair, in_gain, w_in, out_gain, out_bias, w_out, w_gate_out)


def solution(mesh):
    in_specs = (P("row", "col", None), P(), P(), P(), P(), P(), P())
    out_specs = P("row", "col", None)
    return jax.shard_map(local, mesh=mesh, in_specs=in_specs, out_specs=out_specs, check_vma=False)
```

time: 176 us -> 168 us (0.955)
  Pallas kernels: 173 us -> 165 us
    pallas_call x1, Pallas kernels: 173 us -> 165 us  [local(): pl.pallas_call(kernel, out_shape=jax.ShapeDtypeStruct(pair.shape, BF16),...]
where the time goes in v5:
time: 168 us
  Pallas kernels  165 us (98%)
  local copies, waits for them, and re-layouts  2.26 us (1%)
    pallas_call x1, Pallas kernels, local(): pl.pallas_call(kernel, out_shape=jax.ShapeDtypeStruct(pair.shape, BF16),...  165 us

profile of v5, /device:TPU:1, one launch (start us, length us, event | category | flops | bytes accessed | tf_op | source)
XLA Modules:
  0.0 167.7 jit_solution(956006886400891869)
XLA Ops:
  0.0 165.4 %triangles.1 = bf16[128,32,128]{2,1,0:T(8,128)(2,1)} custom-call(bf16[128,32,128]{2,1,0:T(8,128)(2,1)} %pair.1, f32[2,128]{1,0:T(2,128)} %in_gain.1, bf16[2,128,512]{2,1,0:T(8,128)(2,1)} %w_in.1, f32[2,128]{1,0:T(2,128)} %out_gain.1, f32[2,128]{1,0:T(2,128)} %out_bias.1, bf16[2,128,128]{2,1,0:T(8,128)(2,1)} %w_out.1, bf16[2,128,128]{2,1,0:T(8,128)(2,1)} %w_gate.1), custom_call_target="tpu_custom_call" | custom-call | tf_op jit(solution)/shard_map/triangles/pallas_call | solution.py:439
  165.4 2.3 %copy.9 = bf16[128,32,128]{2,1,0:T(8,128)(2,1)} copy(bf16[128,32,128]{2,1,0:T(8,128)(2,1)} %triangles.1) | data formatting | bytes 2097152

commit v6 on v5

--- a/solution.py
+++ b/solution.py
@@ -23,6 +23,14 @@
     return z_lo * 4 + x, z_hi * 8 + y * 2 + core
 
 
+def rem(value, by):
+    return lax.rem(value, jnp.int32(by))
+
+
+def div(value, by):
+    return lax.div(value, jnp.int32(by))
+
+
 def sigmoid(values):
     return 0.5 * jnp.tanh(0.5 * values) + 0.5
 
@@ -39,8 +47,8 @@
 
 
 def kernel(
-    pair, in_gain, w_in, out_gain, out_bias, w_out, w_gate, updated,
-    pair_v, out_v, rows, out_rows, z, x_all, gate, staged, gains, wt_in, wt_out, wt_gate,
+    pair, in_gain_hbm, w_in_hbm, out_gain_hbm, out_bias_hbm, w_out_hbm, w_gate_hbm, updated,
+    in_gain, w_in, out_gain, out_bias, w_out, w_gate, pair_v, out_v, rows, out_rows, z, x_all, gate, staged, gains, wt_in, wt_out, wt_gate,
     ab0, ab1, panel0, panel1, swap_b0, swap_b1, swap_a1, product0, product1, home0, home1,
     send_sems, recv_sems, swap_send, swap_recv, back_send, back_recv, line_sems, local_sems,
 ):
@@ -72,8 +80,22 @@
     def half_of(ref, h):
         return ref.at[:, pl.ds(16 * h, 16)]
 
-    arrival = pltpu.make_async_copy(pair, pair_v, local_sems.at[0])
-    arrival.start()
+    arrivals = [
+        pltpu.make_async_copy(source, target, local_sems.at[n])
+        for n, (source, target) in enumerate(
+            (
+                (pair, pair_v),
+                (w_in_hbm, w_in),
+                (in_gain_hbm, in_gain),
+                (out_gain_hbm, out_gain),
+                (out_bias_hbm, out_bias),
+                (w_out_hbm, w_out),
+                (w_gate_hbm, w_gate),
+            )
+        )
+    ]
+    for copy in arrivals:
+        copy.start()
 
     def flip(block):
         return block.astype(F32).T
@@ -154,7 +176,7 @@
                 pl.semaphore_wait(line_sems.at[1], 3)
 
             def spread(s, _, to_outer=to_outer, e=e):
-                to_inner, to_z = (inner + s // 8) % 4, (z_at + s) % 8
+                to_inner, to_z = rem(inner + div(s, 8), 4), rem(z_at + 3 * s, 8)
                 channel = to_outer * 32 + to_inner * 8 + to_z
                 to_x, to_y = (to_outer, to_inner) if u == 0 else (to_inner, to_outer)
 
@@ -164,7 +186,7 @@
                         slot,
                         send,
                         recv,
-                        device_id=device(to_x, to_y, to_z % 2, to_z // 2, z_lo),
+                        device_id=device(to_x, to_y, rem(to_z, 2), div(to_z, 2), z_lo),
                         device_id_type=MESH,
                     ).start()
 
@@ -242,15 +264,18 @@
         part(p, p, 1)
         give_back(0, p, product, home, ((0, 0),), (0, 1))
         copies = [arrive(at) for at in order[2:]]
-        for side in range(2):
-            if side == 1:
-                for copy in copies:
-                    copy.wait()
-            part(p, 1 - p, side)
-            part(1 - p, p, side)
-            part(1 - p, 1 - p, side)
-        for h in range(2):
-            give_back(0, p, product, home, ((0, 1), (1, 0), (1, 1)), (h,))
+        part(p, 1 - p, 0)
+        part(p, 1 - p, 1)
+        give_back(0, p, product, home, ((1, 0),), (0,))
+        part(1 - p, p, 0)
+        part(1 - p, 1 - p, 0)
+        for copy in copies:
+            copy.wait()
+        part(1 - p, p, 1)
+        give_back(0, p, product, home, ((0, 1),), (0,))
+        part(1 - p, 1 - p, 1)
+        give_back(0, p, product, home, ((1, 1),), (0,))
+        give_back(0, p, product, home, ((1, 0), (0, 1), (1, 1)), (1,))
 
     def multiply1(panel, swap_b, swap_a, product, home):
         def left(p):
@@ -304,10 +329,12 @@
         for copy in arrive(order[2]) + arrive(order[3]):
             copy.wait()
         part(p, 1 - p)
+        give_back(1, p, product, home, ((1, 0),), (0,))
         part(1 - p, p)
+        give_back(1, p, product, home, ((0, 1),), (0,))
         part(1 - p, 1 - p)
-        for h in range(2):
-            give_back(1, p, product, home, ((0, 1), (1, 0), (1, 1)), (h,))
+        give_back(1, p, product, home, ((1, 1),), (0,))
+        give_back(1, p, product, home, ((1, 0), (0, 1), (1, 1)), (1,))
 
     def give_back(u, p, product, home, quarters, halves):
         channel = (x * 32 + y * 8 if u == 0 else y * 32 + x * 8) + z_at
@@ -315,9 +342,9 @@
             for of_x, of_y in quarters:
 
                 def one(s, _, h=h, of_x=of_x, of_y=of_y):
-                    to_x = (p + of_x) % 2 + 2 * ((x // 2 + s // 16) % 2)
-                    to_y = 2 * ((p + of_y) % 2) + (y + s // 8) % 2
-                    to_z, to_core = (z_hi + s // 2) % 4, (core + s) % 2
+                    to_x = (p + of_x) % 2 + 2 * rem(x // 2 + div(s, 16), 2)
+                    to_y = 2 * ((p + of_y) % 2) + rem(y + div(s, 8), 2)
+                    to_z, to_core = rem(z_hi + div(s, 2), 4), rem(core + s, 2)
                     to = device(to_x, to_y, core, to_z, to_core)
                     if u == 0:
                         block = product.at[to[1], to_x, h]
@@ -325,7 +352,7 @@
                         block = product.at[to_y, to_z * 2 + to_core, to_x, h]
                     slot = home.at[h, channel]
                     here = jnp.logical_and(to_x == x, to_y == y)
-                    own = jnp.logical_and(jnp.logical_and(s % 8 == 0, straight), here)
+                    own = jnp.logical_and(jnp.logical_and(rem(s, 8) == 0, straight), here)
 
                     @pl.when(own)
                     def _():
@@ -360,8 +387,9 @@
         z[4 * h + n] = block
         x_all[4 * h + n] = (norm(block.astype(F32)) * wide(gains[3 * u])).astype(BF16)
 
+    for copy in arrivals[:3]:
+        copy.wait()
     weights(0)
-    arrival.wait()
     to_rows(pair_v)
 
     def first(n, _):
@@ -370,6 +398,8 @@
 
     lax.fori_loop(0, BLOCKS, first, 0)
     forward(0, 0, ab0, panel0.at[x, col], recv_sems.at[x])
+    for copy in arrivals[3:]:
+        copy.wait()
     late_weights(0)
     gates(0)
     weights(1)
@@ -408,7 +438,7 @@
             return 0
 
         lax.fori_loop(0, 4, leave, 0)
-        copy = pltpu.make_async_copy(half_of(out_v, h), half_of(updated, h), local_sems.at[1 + h])
+        copy = pltpu.make_async_copy(half_of(out_v, h), half_of(updated, h), local_sems.at[7 + h])
         copy.start()
         leaving.append(copy)
 
@@ -432,16 +462,21 @@
 
 
 def local(pair, in_gain, w_in, out_gain, out_bias, w_out, w_gate_out):
-    vmem = pl.BlockSpec(memory_space=pltpu.VMEM)
     anywhere = pl.BlockSpec(memory_space=pl.ANY)
     block = pltpu.VMEM((2, CHIPS, 16, 128), BF16)
     whole = pltpu.VMEM((128, 32, 128), BF16)
     return pl.pallas_call(
         kernel,
         out_shape=jax.ShapeDtypeStruct(pair.shape, BF16),
-        in_specs=[anywhere] + [vmem] * 6,
+        in_specs=[anywhere] * 7,
         out_specs=anywhere,
         scratch_shapes=[
+            pltpu.VMEM((2, 128), F32),
+            pltpu.VMEM((2, 128, 512), BF16),
+            pltpu.VMEM((2, 128), F32),
+            pltpu.VMEM((2, 128), F32),
+            pltpu.VMEM((2, 128, 128), BF16),
+            pltpu.VMEM((2, 128, 128), BF16),
             whole,
             whole,
             pltpu.VMEM((4096, 128), F32),
@@ -472,7 +507,7 @@
             pltpu.SemaphoreType.DMA((2,)),
             pltpu.SemaphoreType.DMA((2, 2)),
             pltpu.SemaphoreType.REGULAR((2,)),
-            pltpu.SemaphoreType.DMA((3,)),
+            pltpu.SemaphoreType.DMA((9,)),
         ],
         compiler_params=pltpu.CompilerParams(
             collective_id=0, has_side_effects=True, vmem_limit_bytes=56 << 20

time: 168 us -> 165 us (0.982)
  Pallas kernels: 165 us -> 163 us
    pallas_call x1, Pallas kernels: 165 us -> 163 us  [local(): pl.pallas_call(kernel, out_shape=jax.ShapeDtypeStruct(pair.shape, BF16),...]
where the time goes in v6:
time: 165 us
  Pallas kernels  163 us (99%)
  local copies, waits for them, and re-layouts  2.26 us (1%)
    pallas_call x1, Pallas kernels, local(): pl.pallas_call(kernel, out_shape=jax.ShapeDtypeStruct(pair.shape, BF16),...  163 us

profile of v6, /device:TPU:1, one launch (start us, length us, event | category | flops | bytes accessed | tf_op | source)
XLA Modules:
  0.0 164.8 jit_solution(9714186539477437900)
XLA Ops:
  0.0 162.5 %triangles.1 = bf16[128,32,128]{2,1,0:T(8,128)(2,1)} custom-call(bf16[128,32,128]{2,1,0:T(8,128)(2,1)} %pair.1, f32[2,128]{1,0:T(2,128)} %in_gain_hbm.1, bf16[2,128,512]{2,1,0:T(8,128)(2,1)} %w_in_hbm.1, f32[2,128]{1,0:T(2,128)} %out_gain_hbm.1, f32[2,128]{1,0:T(2,128)} %out_bias_hbm.1, bf16[2,128,128]{2,1,0:T(8,128)(2,1)} %w_out_hbm.1, ...), custom_call_target="tpu_custom_call" | custom-call | tf_op jit(solution)/shard_map/triangles/pallas_call | solution.py:468
  162.5 2.3 %copy.9 = bf16[128,32,128]{2,1,0:T(8,128)(2,1)} copy(bf16[128,32,128]{2,1,0:T(8,128)(2,1)} %triangles.1) | data formatting | bytes 2097152

commit v7 on v6

--- a/solution.py
+++ b/solution.py
@@ -48,7 +48,7 @@
 
 def kernel(
     pair, in_gain_hbm, w_in_hbm, out_gain_hbm, out_bias_hbm, w_out_hbm, w_gate_hbm, updated,
-    in_gain, w_in, out_gain, out_bias, w_out, w_gate, pair_v, out_v, rows, out_rows, z, x_all, gate, staged, gains, wt_in, wt_out, wt_gate,
+    in_gain, w_in, out_gain, out_bias, w_out, w_gate, pair_v, rows, out_rows, z, x_all, gate, staged, gains, wt_in, wt_out, wt_gate,
     ab0, ab1, panel0, panel1, swap_b0, swap_b1, swap_a1, product0, product1, home0, home1,
     send_sems, recv_sems, swap_send, swap_recv, back_send, back_recv, line_sems, local_sems,
 ):
@@ -76,9 +76,6 @@
     @pl.when(jnp.logical_not(straight))
     def _():
         greet(bar, along_y + along_x + [column[0], partner])
-
-    def half_of(ref, h):
-        return ref.at[:, pl.ds(16 * h, 16)]
 
     arrivals = [
         pltpu.make_async_copy(source, target, local_sems.at[n])
@@ -176,7 +173,7 @@
                 pl.semaphore_wait(line_sems.at[1], 3)
 
             def spread(s, _, to_outer=to_outer, e=e):
-                to_inner, to_z = rem(inner + div(s, 8), 4), rem(z_at + 3 * s, 8)
+                to_inner, to_z = rem(inner + div(s, 8), 4), rem(z_at + 5 * s, 8)
                 channel = to_outer * 32 + to_inner * 8 + to_z
                 to_x, to_y = (to_outer, to_inner) if u == 0 else (to_inner, to_outer)
 
@@ -417,7 +414,6 @@
         forward(1, h, ab1.at[h], slot, recv_sems.at[4 + 4 * h + y])
     gates(1)
     multiply1(panel1, swap_b1, swap_a1, product1, home1)
-    leaving = []
     for h in range(2):
         received(1, h, home1)
 
@@ -432,15 +428,12 @@
 
         def leave(n, _, h=h):
             at = pl.multiple_of(n * 512, 512)
-            out_v[pl.ds(n * 32, 32), 16 * h : 16 * h + 16] = (
+            updated[pl.ds(n * 32, 32), 16 * h : 16 * h + 16] = (
                 out_rows[pl.ds(at, 512), :].astype(BF16).reshape(32, 16, 128)
             )
             return 0
 
         lax.fori_loop(0, 4, leave, 0)
-        copy = pltpu.make_async_copy(half_of(out_v, h), half_of(updated, h), local_sems.at[7 + h])
-        copy.start()
-        leaving.append(copy)
 
     for sent, sem in (
         (ab0, send_sems.at[0]),
@@ -457,9 +450,6 @@
             rest = sent.at[(*chips, 0)]
             pltpu.make_async_copy(rest, rest, sem).wait()
 
-    for copy in leaving:
-        copy.wait()
-
 
 def local(pair, in_gain, w_in, out_gain, out_bias, w_out, w_gate_out):
     anywhere = pl.BlockSpec(memory_space=pl.ANY)
@@ -467,9 +457,9 @@
     whole = pltpu.VMEM((128, 32, 128), BF16)
     return pl.pallas_call(
         kernel,
-        out_shape=jax.ShapeDtypeStruct(pair.shape, BF16),
+        out_shape=pltpu.VMEM(pair.shape, BF16),
         in_specs=[anywhere] * 7,
-        out_specs=anywhere,
+        out_specs=pl.BlockSpec(memory_space=pltpu.VMEM),
         scratch_shapes=[
             pltpu.VMEM((2, 128), F32),
             pltpu.VMEM((2, 128, 512), BF16),
@@ -477,7 +467,6 @@
             pltpu.VMEM((2, 128), F32),
             pltpu.VMEM((2, 128, 128), BF16),
             pltpu.VMEM((2, 128, 128), BF16),
-            whole,
             whole,
             pltpu.VMEM((4096, 128), F32),
             pltpu.VMEM((2048, 128), F32),
@@ -507,7 +496,7 @@
             pltpu.SemaphoreType.DMA((2,)),
             pltpu.SemaphoreType.DMA((2, 2)),
             pltpu.SemaphoreType.REGULAR((2,)),
-            pltpu.SemaphoreType.DMA((9,)),
+            pltpu.SemaphoreType.DMA((7,)),
         ],
         compiler_params=pltpu.CompilerParams(
             collective_id=0, has_side_effects=True, vmem_limit_bytes=56 << 20

time: 165 us -> 162 us (0.982)
  Pallas kernels: 163 us -> 161 us
where the time goes in v7:
time: 162 us
  Pallas kernels  161 us (99%)
    pallas_call x1, Pallas kernels, local(): pl.pallas_call(kernel, out_shape=pltpu.VMEM(pair.shape, BF16), in_specs=[...  161 us

profile of v7, /device:TPU:1, one launch (start us, length us, event | category | flops | bytes accessed | tf_op | source)
XLA Modules:
  0.0 162.3 jit_solution(7783960474482717897)
XLA Ops:
  0.0 161.4 %triangles.1 = bf16[128,32,128]{2,1,0:T(8,128)(2,1)S(1)} custom-call(bf16[128,32,128]{2,1,0:T(8,128)(2,1)} %pair.1, f32[2,128]{1,0:T(2,128)} %in_gain_hbm.1, bf16[2,128,512]{2,1,0:T(8,128)(2,1)} %w_in_hbm.1, f32[2,128]{1,0:T(2,128)} %out_gain_hbm.1, f32[2,128]{1,0:T(2,128)} %out_bias_hbm.1, bf16[2,128,128]{2,1,0:T(8,128)(2,1)} %w_out_hbm.1, ...), custom_call_target="tpu_custom_call" | custom-call | tf_op jit(solution)/shard_map/triangles/pallas_call | solution.py:458
  161.4 1.0 copy.9

commit v8 on v7

--- a/solution.py
+++ b/solution.py
@@ -137,7 +137,7 @@
                     ]
             return 0
 
-        lax.fori_loop(0, tokens // 4, block, 0)
+        lax.fori_loop(0, tokens // 4, block, 0, unroll=2)
         some = 128 // tokens
 
         def pack(d, _):
@@ -393,7 +393,7 @@
         enter(0, 0, n, lanes([take(n * 4 + q, 32).T for q in range(4)]).astype(BF16))
         return 0
 
-    lax.fori_loop(0, BLOCKS, first, 0)
+    lax.fori_loop(0, BLOCKS, first, 0, unroll=4)
     forward(0, 0, ab0, panel0.at[x, col], recv_sems.at[x])
     for copy in arrivals[3:]:
         copy.wait()
@@ -409,7 +409,7 @@
             enter(1, h, n, finish(0, h, n))
             return 0
 
-        lax.fori_loop(0, 4, second, 0)
+        lax.fori_loop(0, 4, second, 0, unroll=4)
         slot = panel1.at[y, z_hi * 2 + core, x, h]
         forward(1, h, ab1.at[h], slot, recv_sems.at[4 + 4 * h + y])
     gates(1)
@@ -424,7 +424,7 @@
                 out_rows[pl.ds(n * 4 + q, 128, stride=16), :] = staged_out
             return 0
 
-        lax.fori_loop(0, 4, last, 0)
+        lax.fori_loop(0, 4, last, 0, unroll=4)
 
         def leave(n, _, h=h):
             at = pl.multiple_of(n * 512, 512)
@@ -433,7 +433,7 @@
             )
             return 0
 
-        lax.fori_loop(0, 4, leave, 0)
+        lax.fori_loop(0, 4, leave, 0, unroll=4)
 
     for sent, sem in (
         (ab0, send_sems.at[0]),

time: 162 us -> 159 us (0.981)
  Pallas kernels: 161 us -> 158 us
    pallas_call x1, Pallas kernels: 161 us -> 158 us  [local(): pl.pallas_call(kernel, out_shape=pltpu.VMEM(pair.shape, BF16), in_specs=[...]
where the time goes in v8:
time: 159 us
  Pallas kernels  158 us (99%)
    pallas_call x1, Pallas kernels, local(): pl.pallas_call(kernel, out_shape=pltpu.VMEM(pair.shape, BF16), in_specs=[...  158 us

profile of v8, /device:TPU:1, one launch (start us, length us, event | category | flops | bytes accessed | tf_op | source)
XLA Modules:
  0.0 159.0 jit_solution(11679115258521473604)
XLA Ops:
  0.0 158.0 %triangles.1 = bf16[128,32,128]{2,1,0:T(8,128)(2,1)S(1)} custom-call(bf16[128,32,128]{2,1,0:T(8,128)(2,1)} %pair.1, f32[2,128]{1,0:T(2,128)} %in_gain_hbm.1, bf16[2,128,512]{2,1,0:T(8,128)(2,1)} %w_in_hbm.1, f32[2,128]{1,0:T(2,128)} %out_gain_hbm.1, f32[2,128]{1,0:T(2,128)} %out_bias_hbm.1, bf16[2,128,128]{2,1,0:T(8,128)(2,1)} %w_out_hbm.1, ...), custom_call_target="tpu_custom_call" | custom-call | tf_op jit(solution)/shard_map/triangles/pallas_call | solution.py:458
  158.0 1.0 copy.9

commit v9 on v8

--- a/solution.py
+++ b/solution.py
@@ -121,7 +121,7 @@
             rows[pl.ds(at, 512), :] = source[pl.ds(n * some, some)].reshape(512, 128).astype(F32)
             return 0
 
-        lax.fori_loop(0, 128 // some, part, 0)
+        lax.fori_loop(0, 128 // some, part, 0, unroll=2)
 
     def projections(u, h, ab, group):
         lhs = wt_in[u, group].reshape(128, 128)
@@ -137,7 +137,7 @@
                     ]
             return 0
 
-        lax.fori_loop(0, tokens // 4, block, 0, unroll=2)
+        lax.fori_loop(0, tokens // 4, block, 0, unroll=4)
         some = 128 // tokens
 
         def pack(d, _):

time: 159 us -> 158 us (level)
  no operation moved by 1% of the time
where the time goes in v9:
time: 158 us
  Pallas kernels  157 us (99%)
    pallas_call x1, Pallas kernels, local(): pl.pallas_call(kernel, out_shape=pltpu.VMEM(pair.shape, BF16), in_specs=[...  157 us

profile of v9, /device:TPU:1, one launch (start us, length us, event | category | flops | bytes accessed | tf_op | source)
XLA Modules:
  0.0 158.2 jit_solution(4558920851414732319)
XLA Ops:
  0.0 157.3 %triangles.1 = bf16[128,32,128]{2,1,0:T(8,128)(2,1)S(1)} custom-call(bf16[128,32,128]{2,1,0:T(8,128)(2,1)} %pair.1, f32[2,128]{1,0:T(2,128)} %in_gain_hbm.1, bf16[2,128,512]{2,1,0:T(8,128)(2,1)} %w_in_hbm.1, f32[2,128]{1,0:T(2,128)} %out_gain_hbm.1, f32[2,128]{1,0:T(2,128)} %out_bias_hbm.1, bf16[2,128,128]{2,1,0:T(8,128)(2,1)} %w_out_hbm.1, ...), custom_call_target="tpu_custom_call" | custom-call | tf_op jit(solution)/shard_map/triangles/pallas_call | solution.py:458
  157.3 1.0 copy.9
